TPU v7x, 512 devices: a whole 4x8x8 slice. The times are simulated.
512 devices in a mesh: ka: 32 (over z_lo, y), grid: 16 (over z_hi, x, core).
Axes of the slice: x: 4, y: 8, z: 8 (z_hi: 2, z_lo: 4; z = z_hi * 4 + z_lo), core: 2. Of those that a mesh axis runs over, the one named last changes fastest.
Arguments:
- wavefunctions: bfloat16 [32, 512, 2, 2048], P('ka', 'grid'), may hold values from -3 to 3
- projectors: bfloat16 [512, 256], replicated, may hold values from -0.25 to 0.25
- support: int32 [32, 16], replicated, may hold values 0 or 1
- proj_counts: int32 [32], replicated, may hold values from 1 to 8
- aug_matrices: float32 [32, 8, 8], replicated, may hold values from -6 to 6
- atom_sites: float32 [32, 3], replicated, may hold values from 0 to 1
- b_vectors: float32 [2, 3], replicated, may hold values from -0.5 to 0.5
- partner: int32 [32, 2], P('ka'), may hold values from 0 to 31, as said below
- lattice_shift: int32 [32, 2, 3], P('ka'), may hold values from -1 to 1
Outputs:
- correlations: bfloat16 [32, 2, 2, 2048, 2048], P('ka', None, None, 'grid')
Inputs may be any that keep to these rules, and one draw needn't show every extreme that they name: For each of the two b-vectors, partner[k, v] - k modulo 32 is the same for every k; the two b-vectors' differences are independent of each other.
All inputs are finite; a program needn't handle non-finite values.
Results may differ from a plain program's by a relative error of at most 0.0057.
Values may be sent and summed in bfloat16 or wider, within the bound.
No kernel may reach another device: no remote copies, remote signals or barrier semaphores. Data moves between devices by JAX's collectives and lax.ppermute only.
A program may use at most 64 MiB of HBM per device.

v0:
```python
import functools
import math

import jax
import jax.numpy as jnp
from jax import lax
from jax.experimental import pallas as pl
from jax.experimental.pallas import tpu as pltpu
from jax.sharding import PartitionSpec as P

SIDE = 16
DEPTH = 96
TWO_PI = 2.0 * math.pi

Z_LO, Y, Z_HI, X, CORE = 4, 8, 2, 4, 2
Z = Z_LO * Z_HI
POINTS = Z_LO * Y
AXES = ("ka", "grid")
SLABS = 16
SLAB_ROWS = 32
PER_ATOM = 8
HIGHEST = lax.Precision.HIGHEST


def flat_id(x, y, z, core):
    return (((z % Z_LO) * Y + y) * Z_HI + z // Z_LO) * (X * CORE) + x * CORE + core


def route(source_of):
    pairs = []
    for x in range(X):
        for y in range(Y):
            for z in range(Z):
                for core in range(CORE):
                    sx, sy, sz, sc = source_of(x, y, z, core)
                    pairs.append(
                        (flat_id(sx % X, sy % Y, sz % Z, sc), flat_id(x, y, z, core))
                    )
    return pairs


def moved(block, source_of):
    return lax.ppermute(block, AXES, route(source_of))


def from_other_core(block):
    return moved(block, lambda x, y, z, core: (x, y, z, 1 - core))


def from_x(block, offset):
    return moved(block, lambda x, y, z, core: (x + offset, y, z, core))


def along_y(lane, steps):
    if steps == 0:
        return lane
    return moved(
        lane,
        lambda x, y, z, core: (x, y + steps, z + (y + steps) // Y, core),
    )


def along_z(lane, steps):
    ahead = lane
    if steps:
        ahead = moved(lane, lambda x, y, z, core: (x, y, z + steps, core))
    return ahead, moved(lane, lambda x, y, z, core: (x, y, z + steps + Z_LO, core))


def near_pieces(held):
    ahead, behind = held
    left_ahead, right_behind = from_x(ahead, -1), from_x(behind, 1)
    return left_ahead, from_x(behind, -1), from_x(ahead, 1), right_behind


def far_pieces(near):
    return from_x(near[0], -1), from_x(near[3], 1)


def dot00(left, right, precision=None):
    return lax.dot_general(
        left,
        right,
        (((0,), (0,)), ((), ())),
        precision=precision,
        preferred_element_type=jnp.float32,
    )


def left_kernel(
    slot_ref,
    b_ref,
    shift_ref,
    own_ref,
    other_ref,
    proj_ref,
    support_ref,
    counts_ref,
    aug_ref,
    sites_ref,
    out_ref,
    real_ref,
    imag_ref,
    masked_ref,
):
    atoms = support_ref.shape[0]
    nproj = proj_ref.shape[1]
    rows = proj_ref.shape[0]
    width = own_ref.shape[1]
    f32 = jnp.float32

    atom_of = lax.broadcasted_iota(jnp.int32, (atoms, nproj), 1) // PER_ATOM
    spread = (atom_of == lax.broadcasted_iota(jnp.int32, (atoms, nproj), 0)).astype(f32)
    reach = dot00(support_ref[...].astype(f32), spread)
    counts = jnp.broadcast_to(counts_ref[...].astype(f32), (8, atoms))
    counts = jnp.dot(counts, spread, preferred_element_type=f32)[0:1]
    slot_id = (lax.broadcasted_iota(jnp.int32, (1, nproj), 1) % PER_ATOM).astype(f32)
    keep = reach * (slot_id < counts - 0.5).astype(f32)
    for s in range(SLABS):
        at = pl.ds(s * SLAB_ROWS, SLAB_ROWS)
        masked_ref[at, :] = (proj_ref[at, :].astype(f32) * keep[s : s + 1, :]).astype(
            jnp.bfloat16
        )
        first = pl.ds(s * 2 * SLAB_ROWS, SLAB_ROWS)
        second = pl.ds(s * 2 * SLAB_ROWS + SLAB_ROWS, SLAB_ROWS)
        real_ref[at, 0:width] = own_ref[first, :]
        real_ref[at, width : 2 * width] = other_ref[first, :]
        imag_ref[at, 0:width] = own_ref[second, :]
        imag_ref[at, width : 2 * width] = other_ref[second, :]

    masked = masked_ref[...]
    proj_real = dot00(masked, real_ref[...]).astype(jnp.bfloat16).astype(f32)
    proj_imag = dot00(masked, imag_ref[...]).astype(jnp.bfloat16).astype(f32)

    pick = (
        lax.broadcasted_iota(jnp.int32, (PER_ATOM, nproj), 1) % PER_ATOM
        == lax.broadcasted_iota(jnp.int32, (PER_ATOM, nproj), 0)
    ).astype(f32)
    tiled = jnp.dot(aug_ref[...], pick, precision=HIGHEST, preferred_element_type=f32)
    same_atom = (
        lax.broadcasted_iota(jnp.int32, (nproj, nproj), 0) // PER_ATOM
        == lax.broadcasted_iota(jnp.int32, (nproj, nproj), 1) // PER_ATOM
    )
    aug = jnp.where(same_atom, tiled, 0.0)
    aug_real = jnp.dot(aug, proj_real, precision=HIGHEST, preferred_element_type=f32)
    aug_imag = jnp.dot(aug, proj_imag, precision=HIGHEST, preferred_element_type=f32)

    sites = jnp.dot(sites_ref[...], spread, precision=HIGHEST, preferred_element_type=f32)
    chunks = rows // 128
    lanes = lax.broadcasted_iota(jnp.int32, (8, 128), 1)
    block = lax.broadcasted_iota(jnp.int32, (8, 128), 0)
    row_ids = block * 128 + lanes
    along_a = (row_ids % SIDE).astype(f32) / SIDE
    along_b = (row_ids // SIDE % SIDE).astype(f32) / SIDE
    along_c = (row_ids // (SIDE * SIDE)).astype(f32) / DEPTH

    for v in range(2):
        q = [b_ref[v, axis] + shift_ref[v, axis].astype(f32) for axis in range(3)]
        theta = TWO_PI * (q[0] * along_a + q[1] * along_b + q[2] * along_c)
        phi = TWO_PI * (q[0] * sites[0:1] + q[1] * sites[1:2] + q[2] * sites[2:3])
        angle = theta
        for part in range(nproj // 128):
            piece = phi[0:1, part * 128 : (part + 1) * 128]
            angle = jnp.where(block == chunks + part, piece, angle)
        cosine = jnp.transpose(jnp.cos(angle))
        sine = jnp.transpose(jnp.sin(angle))
        weights = []
        for part in range(nproj // 128):
            at = slice(part * 128, (part + 1) * 128)
            cos_p = cosine[:, chunks + part : chunks + part + 1]
            sin_p = sine[:, chunks + part : chunks + part + 1]
            weights.append(
                (
                    cos_p * aug_real[at] - sin_p * aug_imag[at],
                    cos_p * aug_imag[at] + sin_p * aug_real[at],
                )
            )
        weight_real = jnp.concatenate([w[0] for w in weights], axis=0)
        weight_imag = jnp.concatenate([w[1] for w in weights], axis=0)

        def spread_rows(weight):
            high = weight.astype(jnp.bfloat16)
            low = (weight - high.astype(f32)).astype(jnp.bfloat16)
            return jnp.dot(masked, high, preferred_element_type=f32) + jnp.dot(
                masked, low, preferred_element_type=f32
            )

        added_real = spread_rows(weight_real)
        added_imag = spread_rows(weight_imag)
        per_chunk = 128 // SLAB_ROWS
        for s in range(SLABS):
            chunk, inside = s // per_chunk, s % per_chunk * SLAB_ROWS
            at = slice(s * SLAB_ROWS, (s + 1) * SLAB_ROWS)
            cos_r = cosine[inside : inside + SLAB_ROWS, chunk : chunk + 1]
            sin_r = sine[inside : inside + SLAB_ROWS, chunk : chunk + 1]
            wave_real = real_ref[at, :].astype(f32)
            wave_imag = imag_ref[at, :].astype(f32)
            left_real = cos_r * wave_real - sin_r * wave_imag + added_real[at]
            left_imag = cos_r * wave_imag + sin_r * wave_real + added_imag[at]
            left_real = left_real.astype(jnp.bfloat16)
            left_imag = left_imag.astype(jnp.bfloat16)
            slot = slot_ref[v, s]
            top, low = pl.ds(0, SLAB_ROWS), pl.ds(SLAB_ROWS, SLAB_ROWS)
            for side in range(2):
                real_half = left_real[:, side * width : (side + 1) * width]
                imag_half = left_imag[:, side * width : (side + 1) * width]
                base = side * 2 * width
                out_ref[v, slot, top, base : base + width] = real_half
                out_ref[v, slot, low, base : base + width] = imag_half
                out_ref[v, slot, top, base + width : base + 2 * width] = -imag_half
                out_ref[v, slot, low, base + width : base + 2 * width] = real_half


def left_operators(slots, b_vectors, shift, own, other, projectors, support, counts, aug, sites):
    rows, nproj = projectors.shape
    width = own.shape[1]
    smem = pl.BlockSpec(memory_space=pltpu.SMEM)
    vmem = pl.BlockSpec(memory_space=pltpu.VMEM)
    return pl.pallas_call(
        left_kernel,
        out_shape=jax.ShapeDtypeStruct((2, SLABS, 2 * SLAB_ROWS, 4 * width), jnp.bfloat16),
        in_specs=[smem] * 3 + [vmem] * 7,
        out_specs=vmem,
        scratch_shapes=[
            pltpu.VMEM((rows, 2 * width), jnp.bfloat16),
            pltpu.VMEM((rows, 2 * width), jnp.bfloat16),
            pltpu.VMEM((rows, nproj), jnp.bfloat16),
        ],
        compiler_params=pltpu.CompilerParams(vmem_limit_bytes=32 * 1024 * 1024),
        cost_estimate=pl.CostEstimate(
            flops=2_000_000_000, bytes_accessed=4 * 1024 * 1024, transcendentals=4096
        ),
        name="left_operators",
    )(slots, b_vectors, shift, own, other, projectors, support, counts, aug, sites)


def product_kernel(left_ref, *refs):
    pieces, (mine_ref, theirs_ref) = refs[:-2], refs[-2:]
    half = mine_ref.shape[0]
    right = jnp.concatenate([piece[...] for piece in pieces], axis=0)
    for side, out_ref in enumerate((mine_ref, theirs_ref)):
        left = left_ref[:, side * half : (side + 1) * half]
        out_ref[...] = dot00(left, right).astype(jnp.bfloat16)


def product(left, pieces):
    depth, wide = left.shape
    columns = pieces[0].shape[1]
    tile = 256
    half = wide // 2
    return pl.pallas_call(
        product_kernel,
        grid=(columns // tile,),
        out_shape=[jax.ShapeDtypeStruct((half, columns), jnp.bfloat16)] * 2,
        in_specs=[pl.BlockSpec((depth, wide), lambda i: (0, 0))]
        + [pl.BlockSpec((p.shape[0], tile), lambda i: (0, i)) for p in pieces],
        out_specs=[pl.BlockSpec((half, tile), lambda i: (0, i))] * 2,
        compiler_params=pltpu.CompilerParams(vmem_limit_bytes=32 * 1024 * 1024),
        cost_estimate=pl.CostEstimate(
            flops=2 * depth * wide * columns,
            bytes_accessed=5 * 1024 * 1024,
            transcendentals=0,
        ),
        name="product",
    )(left, *pieces)


def body(
    wavefunctions,
    projectors,
    support,
    proj_counts,
    aug_matrices,
    atom_sites,
    b_vectors,
    partner,
    lattice_shift,
):
    waves = wavefunctions[0]
    row_count, _, bands = waves.shape
    half_bands = bands // CORE
    point, member = lax.axis_index("ka"), lax.axis_index("grid")
    core, x, z_hi = member % CORE, member // CORE % X, member // (CORE * X)
    y, z_lo = point % Y, point // Y
    z = z_hi * Z_LO + z_lo
    distances = [(partner[0, v] - point) % POINTS for v in range(2)]

    slab = jnp.transpose(waves, (1, 0, 2)).reshape(2 * row_count, bands)
    low, high = slab[:, :half_bands], slab[:, half_bands:]
    kept = jnp.where(core == 0, low, high)
    given = jnp.where(core == 0, high, low)
    lane = jnp.concatenate([kept, from_other_core(given)], axis=0)

    steps_y = [d % Y for d in distances]
    steps_z = [d // Y for d in distances]

    def second_stage(y_second, z_first, lane, moved_first):
        return along_y(lane, y_second), along_z(moved_first, z_first)

    def third_stage(z_second, moved_second, held_first, slab):
        held_second = along_z(moved_second, z_second)
        near_first = near_pieces(held_first)
        own = lax.all_to_all(slab, "grid", split_axis=1, concat_axis=0, tiled=True)
        return held_second, near_first, own

    moved_first = lax.switch(
        steps_y[0], [functools.partial(along_y, steps=s) for s in range(Y)], lane
    )
    moved_second, held_first = lax.switch(
        steps_y[1] * Z_LO + steps_z[0],
        [
            functools.partial(second_stage, y_second, z_first)
            for y_second in range(Y)
            for z_first in range(Z_LO)
        ],
        lane,
        moved_first,
    )
    held_second, near_first, own = lax.switch(
        steps_z[1],
        [functools.partial(third_stage, s) for s in range(Z_LO)],
        moved_second,
        held_first,
        slab,
    )
    other = from_other_core(own)
    slab_ids = jnp.arange(SLABS, dtype=jnp.int32)
    places = []
    for v in range(2):
        ahead_hi = (z + steps_z[v] + (y + steps_y[v]) // Y) % Z // Z_LO
        is_behind = (slab_ids // (CORE * X) != ahead_hi).astype(jnp.int32)
        step = (slab_ids // CORE % X - x) % X
        piece = jnp.where(step == 3, 1, jnp.where(step == 0, 0, step + 1))
        is_other = (slab_ids % CORE != core).astype(jnp.int32)
        places.append(piece * 4 + is_behind * 2 + is_other)
    slots = jnp.stack(places).astype(jnp.int32)
    left = left_operators(
        slots,
        b_vectors,
        lattice_shift[0],
        own,
        other,
        projectors,
        support,
        proj_counts.reshape(1, -1),
        jnp.transpose(aug_matrices, (0, 2, 1)).reshape(-1, PER_ATOM),
        jnp.transpose(atom_sites),
    )
    left = left.reshape(2, left.shape[1] * left.shape[2], left.shape[3])

    far_first = far_pieces(near_first)
    near_second = near_pieces(held_second)
    mine_first, theirs_first = product(left[0], held_first + near_first + far_first)
    got_first = from_other_core(theirs_first)
    far_second = far_pieces(near_second)
    mine_second, theirs_second = product(left[1], held_second + near_second + far_second)
    got_second = from_other_core(theirs_second)

    def joined(mine, got):
        return jnp.concatenate(
            [jnp.where(core == 0, mine, got), jnp.where(core == 0, got, mine)], axis=1
        )

    final = jnp.stack([joined(mine_first, got_first), joined(mine_second, got_second)])
    return final.reshape(1, 2, 2, bands // SLABS, bands)


def solution(mesh):
    in_specs = (
        P("ka", "grid", None, None),
        P(),
        P(),
        P(),
        P(),
        P(),
        P(),
        P("ka", None),
        P("ka", None, None),
    )
    out_specs = P("ka", None, None, "grid", None)
    return jax.shard_map(body, mesh=mesh, in_specs=in_specs, out_specs=out_specs, check_vma=False)
```

profile of v0, /device:TPU:1, one launch (start us, length us, event | category | flops | bytes accessed | tf_op | source)
XLA Modules:
  0.0 137.6 jit_solution(10076662280299673407)
XLA Ops:
  0.0 1.0 copy.21
  1.1 8.8 %collective-permute-start.114 = (bf16[64,1024]{1,0:T(8,128)(2,1)S(1)}, bf16[64,1024]{1,0:T(8,128)(2,1)S(1)}, u32[]{:S(2)}, u32[]{:S(2)}) collective-permute-start(bf16[64,1024]{1,0:T(8,128)(2,1)S(1)} %get-tuple-element.313), channel_id=1, source_target_pairs={{1,0},{0,1},{129,128},{128,129},{257,256},{256,257},{385,384},{384... | collective-permute-start | bytes 393224 | tf_op jit(solution)/shard_map/ppermute | solution.py:43
  9.9 1.3 fusion.9
  12.5 0.7 conditional.3
  12.5 0.7 copy.32
  13.2 30.2 %conditional.4 = (bf16[128,1024]{1,0:T(8,128)(2,1)S(1)}, bf16[128,1024]{1,0:T(8,128)(2,1)}, bf16[128,1024]{1,0:T(8,128)(2,1)}) conditional(s32[]{:T(128)} %clamp.10, (bf16[128,1024]{1,0:T(8,128)(2,1)}, bf16[128,1024]{1,0:T(8,128)(2,1)S(1)}) %tuple.182, (bf16[128,1024]{1,0:T(8,128)(2,1)}, ...), branch_computations={%region_8.9_spmd, %region_9.10_spmd, %region_10.11_spmd, %region_1... | conditional | bytes 3670160 | solution.py:309
  13.2 9.0 %collective-permute-start.27 = (bf16[128,1024]{1,0:T(8,128)(2,1)S(1)}, bf16[128,1024]{1,0:T(8,128)(2,1)S(1)}, u32[]{:S(2)}, u32[]{:S(2)}) collective-permute-start(bf16[128,1024]{1,0:T(8,128)(2,1)S(1)} %get-tuple-element.208), channel_id=1, source_target_pairs={{32,0},{33,1},{160,128},{161,129},{288,256},{289,257},{416,384},{4... | collective-permute-start | bytes 786440 | tf_op jit(solution)/shard_map/cond/branch_9_fun/ppermute | solution.py:43
  22.2 2.2 %collective-permute-start.28 = (bf16[128,1024]{1,0:T(8,128)(2,1)}, bf16[128,1024]{1,0:T(8,128)(2,1)}, u32[]{:S(2)}, u32[]{:S(2)}) collective-permute-start(bf16[128,1024]{1,0:T(8,128)(2,1)} %get-tuple-element.209), channel_id=1, source_target_pairs={{128,0},{129,1},{256,128},{257,129},{384,256},{385,257},{8,384},{9... | collective-permute-start | bytes 786440 | tf_op jit(solution)/shard_map/cond/branch_9_fun/ppermute | solution.py:43
  24.4 1.9 %collective-permute-start.29 = (bf16[128,1024]{1,0:T(8,128)(2,1)}, bf16[128,1024]{1,0:T(8,128)(2,1)}, u32[]{:S(2)}, u32[]{:S(2)}) collective-permute-start(bf16[128,1024]{1,0:T(8,128)(2,1)} %get-tuple-element.209), channel_id=1, source_target_pairs={{136,0},{137,1},{264,128},{265,129},{392,256},{393,257},{0,384},{1... | collective-permute-start | bytes 786440 | tf_op jit(solution)/shard_map/cond/branch_9_fun/ppermute | solution.py:43
  26.3 7.2 %collective-permute-done.27 = bf16[128,1024]{1,0:T(8,128)(2,1)S(1)} collective-permute-done((bf16[128,1024]{1,0:T(8,128)(2,1)S(1)}, bf16[128,1024]{1,0:T(8,128)(2,1)S(1)}, u32[]{:S(2)}, u32[]{:S(2)}) %collective-permute-start.27) | collective-permute-done | bytes 262176 | tf_op jit(solution)/shard_map/cond/branch_9_fun/ppermute | solution.py:43
  33.6 9.9 %collective-permute-done.29 = bf16[128,1024]{1,0:T(8,128)(2,1)} collective-permute-done((bf16[128,1024]{1,0:T(8,128)(2,1)}, bf16[128,1024]{1,0:T(8,128)(2,1)}, u32[]{:S(2)}, u32[]{:S(2)}) %collective-permute-start.29) | collective-permute-done | bytes 262176 | tf_op jit(solution)/shard_map/cond/branch_9_fun/ppermute | solution.py:43
  43.5 0.0 copy-start.4
  43.5 38.2 %conditional.5 = (bf16[128,1024]{1,0:T(8,128)(2,1)}, bf16[128,1024]{1,0:T(8,128)(2,1)}, bf16[128,1024]{1,0:T(8,128)(2,1)}, bf16[128,1024]{1,0:T(8,128)(2,1)}, bf...) conditional(s32[]{:T(128)} %clamp.9, ...), branch_computations={%region_40.41_spmd, %region_41.42_spmd, %region_42.43_spmd, %regio... | conditional | bytes 7602504 | solution.py:319
  43.6 2.1 %collective-permute-start.108 = (bf16[128,1024]{1,0:T(8,128)(2,1)S(1)}, bf16[128,1024]{1,0:T(8,128)(2,1)}, u32[]{:S(2)}, u32[]{:S(2)}) collective-permute-start(bf16[128,1024]{1,0:T(8,128)(2,1)S(1)} %get-tuple-element.266), channel_id=1, source_target_pairs={{384,0},{385,1},{8,128},{9,129},{136,256},{137,257},{264,384},{265... | collective-permute-start | bytes 786440 | tf_op jit(solution)/shard_map/cond/branch_3_fun/ppermute | solution.py:43
  45.6 0.8 copy_bitcast_fusion.3
  46.4 14.8 %all-to-all-start.3 = ((bf16[64,16,128]{2,0,1:T(8,128)(2,1)}), bf16[64,16,128]{2,0,1:T(8,128)(2,1)}, u32[]{:S(2)}, u32[]{:S(2)}) async-start(bf16[64,16,128]{2,0,1:T(8,128)(2,1)} %copy_bitcast_fusion.3), calls=%async_computation.3 | async-start | bytes 524288 | tf_op jit(solution)/shard_map/cond/branch_3_fun/all_to_all | solution.py:303
  61.2 1.9 %collective-permute-start.109 = (bf16[128,1024]{1,0:T(8,128)(2,1)S(1)}, bf16[128,1024]{1,0:T(8,128)(2,1)}, u32[]{:S(2)}, u32[]{:S(2)}) collective-permute-start(bf16[128,1024]{1,0:T(8,128)(2,1)S(1)} %get-tuple-element.266), channel_id=1, source_target_pairs={{392,0},{393,1},{0,128},{1,129},{128,256},{129,257},{256,384},{257... | collective-permute-start | bytes 786440 | tf_op jit(solution)/shard_map/cond/branch_3_fun/ppermute | solution.py:43
  63.1 3.3 %collective-permute-start.110 = (bf16[128,1024]{1,0:T(8,128)(2,1)}, bf16[128,1024]{1,0:T(8,128)(2,1)}, u32[]{:S(2)}, u32[]{:S(2)}) collective-permute-start(bf16[128,1024]{1,0:T(8,128)(2,1)} %get-tuple-element.267), channel_id=1, source_target_pairs={{6,0},{7,1},{134,128},{135,129},{262,256},{263,257},{390,384},{391... | collective-permute-start | bytes 786440 | tf_op jit(solution)/shard_map/cond/branch_3_fun/ppermute | solution.py:43
  66.4 3.2 %collective-permute-start.112 = (bf16[128,1024]{1,0:T(8,128)(2,1)}, bf16[128,1024]{1,0:T(8,128)(2,1)}, u32[]{:S(2)}, u32[]{:S(2)}) collective-permute-start(bf16[128,1024]{1,0:T(8,128)(2,1)} %get-tuple-element.267), channel_id=1, source_target_pairs={{2,0},{3,1},{130,128},{131,129},{258,256},{259,257},{386,384},{387... | collective-permute-start | bytes 786440 | tf_op jit(solution)/shard_map/cond/branch_3_fun/ppermute | solution.py:43
  69.6 2.1 %collective-permute-start.111 = (bf16[128,1024]{1,0:T(8,128)(2,1)}, bf16[128,1024]{1,0:T(8,128)(2,1)}, u32[]{:S(2)}, u32[]{:S(2)}) collective-permute-start(bf16[128,1024]{1,0:T(8,128)(2,1)} %get-tuple-element.268), channel_id=1, source_target_pairs={{6,0},{7,1},{134,128},{135,129},{262,256},{263,257},{390,384},{391... | collective-permute-start | bytes 786440 | tf_op jit(solution)/shard_map/cond/branch_3_fun/ppermute | solution.py:43
  71.7 4.4 %collective-permute-start.113 = (bf16[128,1024]{1,0:T(8,128)(2,1)}, bf16[128,1024]{1,0:T(8,128)(2,1)}, u32[]{:S(2)}, u32[]{:S(2)}) collective-permute-start(bf16[128,1024]{1,0:T(8,128)(2,1)} %get-tuple-element.268), channel_id=1, source_target_pairs={{2,0},{3,1},{130,128},{131,129},{258,256},{259,257},{386,384},{387... | collective-permute-start | bytes 786440 | tf_op jit(solution)/shard_map/cond/branch_3_fun/ppermute | solution.py:43
  76.2 5.0 %collective-permute-done.111 = bf16[128,1024]{1,0:T(8,128)(2,1)} collective-permute-done((bf16[128,1024]{1,0:T(8,128)(2,1)}, bf16[128,1024]{1,0:T(8,128)(2,1)}, u32[]{:S(2)}, u32[]{:S(2)}) %collective-permute-start.111) | collective-permute-done | bytes 262176 | tf_op jit(solution)/shard_map/cond/branch_3_fun/ppermute | solution.py:43
  81.2 0.5 collective-permute-done.113
  81.7 3.4 %collective-permute-start.115 = (bf16[1024,128]{1,0:T(8,128)(2,1)}, bf16[1024,128]{1,0:T(8,128)(2,1)S(1)}, u32[]{:S(2)}, u32[]{:S(2)}) collective-permute-start(bf16[1024,128]{1,0:T(8,128)(2,1)} %get-tuple-element.305.own_ref), channel_id=1, source_target_pairs={{1,0},{0,1},{129,128},{128,129},{257,256},{256,257},{385,384},{384... | collective-permute-start | bytes 786440 | tf_op jit(solution)/shard_map/ppermute | solution.py:43
  85.3 0.1 copy.22
  85.5 0.1 copy.23.support_ref
  85.6 3.2 %collective-permute-start.116 = (bf16[128,1024]{1,0:T(8,128)(2,1)}, bf16[128,1024]{1,0:T(8,128)(2,1)S(1)}, u32[]{:S(2)}, u32[]{:S(2)}) collective-permute-start(bf16[128,1024]{1,0:T(8,128)(2,1)} %get-tuple-element.300.refs_2_), channel_id=1, source_target_pairs={{6,0},{7,1},{134,128},{135,129},{262,256},{263,257},{390,384},{391... | collective-permute-start | bytes 786440 | tf_op jit(solution)/shard_map/ppermute | solution.py:43
  88.8 3.8 %collective-permute-start.117 = (bf16[128,1024]{1,0:T(8,128)(2,1)}, bf16[128,1024]{1,0:T(8,128)(2,1)S(1)}, u32[]{:S(2)}, u32[]{:S(2)}) collective-permute-start(bf16[128,1024]{1,0:T(8,128)(2,1)} %get-tuple-element.303.refs_5_), channel_id=1, source_target_pairs={{2,0},{3,1},{130,128},{131,129},{258,256},{259,257},{386,384},{387... | collective-permute-start | bytes 786440 | tf_op jit(solution)/shard_map/ppermute | solution.py:43
  92.6 1.9 %collective-permute-start.119 = (bf16[128,1024]{1,0:T(8,128)(2,1)}, bf16[128,1024]{1,0:T(8,128)(2,1)S(1)}, u32[]{:S(2)}, u32[]{:S(2)}) collective-permute-start(bf16[128,1024]{1,0:T(8,128)(2,1)} %get-tuple-element.298.refs_0_), channel_id=1, source_target_pairs={{6,0},{7,1},{134,128},{135,129},{262,256},{263,257},{390,384},{391... | collective-permute-start | bytes 786440 | tf_op jit(solution)/shard_map/ppermute | solution.py:43
  94.5 4.6 %collective-permute-start.122 = (bf16[128,1024]{1,0:T(8,128)(2,1)}, bf16[128,1024]{1,0:T(8,128)(2,1)S(1)}, u32[]{:S(2)}, u32[]{:S(2)}) collective-permute-start(bf16[128,1024]{1,0:T(8,128)(2,1)} %get-tuple-element.299.refs_1_), channel_id=1, source_target_pairs={{2,0},{3,1},{130,128},{131,129},{258,256},{259,257},{386,384},{387... | collective-permute-start | bytes 786440 | tf_op jit(solution)/shard_map/ppermute | solution.py:43
  99.1 3.8 %left_operators.1 = bf16[2,16,64,512]{3,2,1,0:T(8,128)(2,1)S(1)} custom-call(s32[2,16]{1,0:T(2,128)S(1)} %pad_add_fusion.slot_ref, f32[2,3]{1,0:T(2,128)S(1)} %copy-done.2, s32[2,3]{1,0:T(2,128)S(1)} %bitcast.51, bf16[1024,128]{1,0:T(8,128)(2,1)} %get-tuple-element.305.own_ref, bf16[1024,128]{1,0:T(8,128)(2,1)S(1)} %collective-permute-done.115.other_ref, ...), custom_call_target="tpu_custom_call" | custom-call | flops 2000000000 | bytes 4194304 | tf_op jit(solution)/shard_map/left_operators/pallas_call | solution.py:219
  103.0 0.1 fusion.8
  103.1 3.6 %product.2 = (bf16[256,1024]{1,0:T(8,128)(2,1)S(1)}, bf16[256,1024]{1,0:T(8,128)(2,1)S(1)}) custom-call(bf16[1024,512]{1,0:T(8,128)(2,1)S(1)} %bitcast.48, bf16[128,1024]{1,0:T(8,128)(2,1)} %get-tuple-element.285.refs_0_, bf16[128,1024]{1,0:T(8,128)(2,1)} %get-tuple-element.286.refs_1_, bf16[128,1024]{1,0:T(8,128)(2,1)} %get-tuple-element.300.refs_2_, ...), custom_call_target="tpu_custom_call" | custom-call | flops 1073741824 | bytes 5242880 | tf_op jit(solution)/shard_map/product/pallas_call | solution.py:251
  106.8 2.8 %collective-permute-start.118 = (bf16[256,1024]{1,0:T(8,128)(2,1)S(1)}, bf16[256,1024]{1,0:T(8,128)(2,1)S(1)}, u32[]{:S(2)}, u32[]{:S(2)}) collective-permute-start(bf16[256,1024]{1,0:T(8,128)(2,1)S(1)} %get-tuple-element.293), channel_id=1, source_target_pairs={{1,0},{0,1},{129,128},{128,129},{257,256},{256,257},{385,384},{384... | collective-permute-start | bytes 1572872 | tf_op jit(solution)/shard_map/ppermute | solution.py:43
  109.6 1.9 %collective-permute-start.120 = (bf16[128,1024]{1,0:T(8,128)(2,1)}, bf16[128,1024]{1,0:T(8,128)(2,1)S(1)}, u32[]{:S(2)}, u32[]{:S(2)}) collective-permute-start(bf16[128,1024]{1,0:T(8,128)(2,1)} %get-tuple-element.299.refs_1_), channel_id=1, source_target_pairs={{6,0},{7,1},{134,128},{135,129},{262,256},{263,257},{390,384},{391... | collective-permute-start | bytes 786440 | tf_op jit(solution)/shard_map/ppermute | solution.py:43
  111.5 4.6 %collective-permute-start.121 = (bf16[128,1024]{1,0:T(8,128)(2,1)}, bf16[128,1024]{1,0:T(8,128)(2,1)S(1)}, u32[]{:S(2)}, u32[]{:S(2)}) collective-permute-start(bf16[128,1024]{1,0:T(8,128)(2,1)} %get-tuple-element.298.refs_0_), channel_id=1, source_target_pairs={{2,0},{3,1},{130,128},{131,129},{258,256},{259,257},{386,384},{387... | collective-permute-start | bytes 786440 | tf_op jit(solution)/shard_map/ppermute | solution.py:43
  116.1 1.9 %collective-permute-start.123 = (bf16[128,1024]{1,0:T(8,128)(2,1)S(1)}, bf16[128,1024]{1,0:T(8,128)(2,1)S(1)}, u32[]{:S(2)}, u32[]{:S(2)}) collective-permute-start(bf16[128,1024]{1,0:T(8,128)(2,1)S(1)} %collective-permute-done.119.refs_2_), channel_id=1, source_target_pairs={{6,0},{7,1},{134,128},{135,129},{262,256},{263,257},{390,384},{391... | collective-permute-start | bytes 786440 | tf_op jit(solution)/shard_map/ppermute | solution.py:43
  118.0 4.6 %collective-permute-start.124 = (bf16[128,1024]{1,0:T(8,128)(2,1)S(1)}, bf16[128,1024]{1,0:T(8,128)(2,1)S(1)}, u32[]{:S(2)}, u32[]{:S(2)}) collective-permute-start(bf16[128,1024]{1,0:T(8,128)(2,1)S(1)} %collective-permute-done.122.refs_5_), channel_id=1, source_target_pairs={{2,0},{3,1},{130,128},{131,129},{258,256},{259,257},{386,384},{387... | collective-permute-start | bytes 786440 | tf_op jit(solution)/shard_map/ppermute | solution.py:43
  122.6 3.9 %collective-permute-done.123.refs_6_ = bf16[128,1024]{1,0:T(8,128)(2,1)S(1)} collective-permute-done((bf16[128,1024]{1,0:T(8,128)(2,1)S(1)}, bf16[128,1024]{1,0:T(8,128)(2,1)S(1)}, u32[]{:S(2)}, u32[]{:S(2)}) %collective-permute-start.123) | collective-permute-done | bytes 262176 | tf_op jit(solution)/shard_map/ppermute | solution.py:43
  126.5 0.9 collective-permute-done.124.refs_7_
  127.3 3.4 %product.3 = (bf16[256,1024]{1,0:T(8,128)(2,1)S(1)}, bf16[256,1024]{1,0:T(8,128)(2,1)S(1)}) custom-call(bf16[1024,512]{1,0:T(8,128)(2,1)S(1)} %bitcast.47, bf16[128,1024]{1,0:T(8,128)(2,1)} %get-tuple-element.298.refs_0_, bf16[128,1024]{1,0:T(8,128)(2,1)} %get-tuple-element.299.refs_1_, bf16[128,1024]{1,0:T(8,128)(2,1)S(1)} %collective-permute-done.119.refs_2_, ...), custom_call_target="tpu_custom_call" | custom-call | flops 1073741824 | bytes 5242880 | tf_op jit(solution)/shard_map/product/pallas_call | solution.py:251
  130.7 3.7 %collective-permute-start.125 = (bf16[256,1024]{1,0:T(8,128)(2,1)S(1)}, bf16[256,1024]{1,0:T(8,128)(2,1)S(1)}, u32[]{:S(2)}, u32[]{:S(2)}) collective-permute-start(bf16[256,1024]{1,0:T(8,128)(2,1)S(1)} %get-tuple-element.297), channel_id=1, source_target_pairs={{1,0},{0,1},{129,128},{128,129},{257,256},{256,257},{385,384},{384... | collective-permute-start | bytes 1572872 | tf_op jit(solution)/shard_map/ppermute | solution.py:43
  134.4 0.1 broadcast_select_fusion.3
  134.5 0.1 pad_maximum_fusion.1
  134.6 1.3 collective-permute-done.125
  135.9 0.1 broadcast_select_fusion.1
  136.0 0.1 pad_maximum_fusion.2
  136.1 1.5 %pad_maximum_fusion = bf16[1,2,2,128,2048]{4,3,2,1,0:T(8,128)(2,1)} fusion(bf16[1,1,2,128,2048]{4,3,2,1,0:T(8,128)(2,1)S(1)} %bitcast.59, bf16[1,1,2,128,2048]{4,3,2,1,0:T(8,128)(2,1)S(1)} %bitcast.58), kind=kLoop, calls=%fused_computation.4 | loop fusion | flops 1048576 | bytes 4194304 | tf_op jit(solution)/shard_map/stack | solution.py:364
  (33 shorter events, 0.2 us)
Async XLA Ops:
  1.1 11.4 %collective-permute-start.114 = (bf16[64,1024]{1,0:T(8,128)(2,1)S(1)}, bf16[64,1024]{1,0:T(8,128)(2,1)S(1)}, u32[]{:S(2)}, u32[]{:S(2)}) collective-permute-start(bf16[64,1024]{1,0:T(8,128)(2,1)S(1)} %get-tuple-element.313), channel_id=1, source_target_pairs={{1,0},{0,1},{129,128},{128,129},{257,256},{256,257},{385,384},{384... | collective-permute-start | bytes 393224 | tf_op jit(solution)/shard_map/ppermute | solution.py:43
  13.2 20.3 %collective-permute-start.27 = (bf16[128,1024]{1,0:T(8,128)(2,1)S(1)}, bf16[128,1024]{1,0:T(8,128)(2,1)S(1)}, u32[]{:S(2)}, u32[]{:S(2)}) collective-permute-start(bf16[128,1024]{1,0:T(8,128)(2,1)S(1)} %get-tuple-element.208), channel_id=1, source_target_pairs={{32,0},{33,1},{160,128},{161,129},{288,256},{289,257},{416,384},{4... | collective-permute-start | bytes 786440 | tf_op jit(solution)/shard_map/cond/branch_9_fun/ppermute | solution.py:43
  22.2 11.4 %collective-permute-start.28 = (bf16[128,1024]{1,0:T(8,128)(2,1)}, bf16[128,1024]{1,0:T(8,128)(2,1)}, u32[]{:S(2)}, u32[]{:S(2)}) collective-permute-start(bf16[128,1024]{1,0:T(8,128)(2,1)} %get-tuple-element.209), channel_id=1, source_target_pairs={{128,0},{129,1},{256,128},{257,129},{384,256},{385,257},{8,384},{9... | collective-permute-start | bytes 786440 | tf_op jit(solution)/shard_map/cond/branch_9_fun/ppermute | solution.py:43
  24.4 19.1 %collective-permute-start.29 = (bf16[128,1024]{1,0:T(8,128)(2,1)}, bf16[128,1024]{1,0:T(8,128)(2,1)}, u32[]{:S(2)}, u32[]{:S(2)}) collective-permute-start(bf16[128,1024]{1,0:T(8,128)(2,1)} %get-tuple-element.209), channel_id=1, source_target_pairs={{136,0},{137,1},{264,128},{265,129},{392,256},{393,257},{0,384},{1... | collective-permute-start | bytes 786440 | tf_op jit(solution)/shard_map/cond/branch_9_fun/ppermute | solution.py:43
  43.5 41.8 %copy-start.5 = (f32[32,8,8]{0,2,1:T(8,128)S(1)}, f32[32,8,8]{0,2,1:T(8,128)}, u32[]{:S(2)}) copy-start(f32[32,8,8]{0,2,1:T(8,128)} %param.57) | copy-start | bytes 24580
  43.5 42.0 %copy-start.6 = (s32[32,16]{0,1:T(8,128)S(1)}, s32[32,16]{0,1:T(8,128)}, u32[]{:S(2)}) copy-start(s32[32,16]{0,1:T(8,128)} %param.55) | copy-start | bytes 6148
  43.5 55.6 %copy-start = (bf16[512,256]{1,0:T(8,128)(2,1)S(1)}, bf16[512,256]{1,0:T(8,128)(2,1)}, u32[]{:S(2)}) copy-start(bf16[512,256]{1,0:T(8,128)(2,1)} %proj_ref.1) | copy-start | bytes 786436
  43.5 55.6 %copy-start.1 = (f32[32,3]{0,1:T(4,128)S(1)}, f32[32,3]{0,1:T(4,128)}, u32[]{:S(2)}) copy-start(f32[32,3]{0,1:T(4,128)} %param.58) | copy-start | bytes 1156
  43.5 55.6 %copy-start.2 = (f32[2,3]{1,0:T(2,128)S(1)}, f32[2,3]{1,0:T(2,128)}, u32[]{:S(2)}) copy-start(f32[2,3]{1,0:T(2,128)} %b_ref.1) | copy-start | bytes 76
  43.5 55.6 %copy-start.3 = (s32[1,2,3]{2,1,0:T(2,128)S(1)}, s32[1,2,3]{2,1,0:T(2,128)}, u32[]{:S(2)}) copy-start(s32[1,2,3]{2,1,0:T(2,128)} %param.61) | copy-start | bytes 76
  43.5 55.6 %copy-start.4 = (s32[32]{0:T(128)S(1)}, s32[32]{0:T(128)}, u32[]{:S(2)}) copy-start(s32[32]{0:T(128)} %param.56) | copy-start | bytes 388
  43.6 28.2 %collective-permute-start.108 = (bf16[128,1024]{1,0:T(8,128)(2,1)S(1)}, bf16[128,1024]{1,0:T(8,128)(2,1)}, u32[]{:S(2)}, u32[]{:S(2)}) collective-permute-start(bf16[128,1024]{1,0:T(8,128)(2,1)S(1)} %get-tuple-element.266), channel_id=1, source_target_pairs={{384,0},{385,1},{8,128},{9,129},{136,256},{137,257},{264,384},{265... | collective-permute-start | bytes 786440 | tf_op jit(solution)/shard_map/cond/branch_3_fun/ppermute | solution.py:43
  46.4 35.3 %all-to-all-start.3 = ((bf16[64,16,128]{2,0,1:T(8,128)(2,1)}), bf16[64,16,128]{2,0,1:T(8,128)(2,1)}, u32[]{:S(2)}, u32[]{:S(2)}) async-start(bf16[64,16,128]{2,0,1:T(8,128)(2,1)} %copy_bitcast_fusion.3), calls=%async_computation.3 | async-start | bytes 524288 | tf_op jit(solution)/shard_map/cond/branch_3_fun/all_to_all | solution.py:303
  61.2 15.0 %collective-permute-start.109 = (bf16[128,1024]{1,0:T(8,128)(2,1)S(1)}, bf16[128,1024]{1,0:T(8,128)(2,1)}, u32[]{:S(2)}, u32[]{:S(2)}) collective-permute-start(bf16[128,1024]{1,0:T(8,128)(2,1)S(1)} %get-tuple-element.266), channel_id=1, source_target_pairs={{392,0},{393,1},{0,128},{1,129},{128,256},{129,257},{256,384},{257... | collective-permute-start | bytes 786440 | tf_op jit(solution)/shard_map/cond/branch_3_fun/ppermute | solution.py:43
  63.1 13.0 %collective-permute-start.110 = (bf16[128,1024]{1,0:T(8,128)(2,1)}, bf16[128,1024]{1,0:T(8,128)(2,1)}, u32[]{:S(2)}, u32[]{:S(2)}) collective-permute-start(bf16[128,1024]{1,0:T(8,128)(2,1)} %get-tuple-element.267), channel_id=1, source_target_pairs={{6,0},{7,1},{134,128},{135,129},{262,256},{263,257},{390,384},{391... | collective-permute-start | bytes 786440 | tf_op jit(solution)/shard_map/cond/branch_3_fun/ppermute | solution.py:43
  66.4 14.8 %collective-permute-start.112 = (bf16[128,1024]{1,0:T(8,128)(2,1)}, bf16[128,1024]{1,0:T(8,128)(2,1)}, u32[]{:S(2)}, u32[]{:S(2)}) collective-permute-start(bf16[128,1024]{1,0:T(8,128)(2,1)} %get-tuple-element.267), channel_id=1, source_target_pairs={{2,0},{3,1},{130,128},{131,129},{258,256},{259,257},{386,384},{387... | collective-permute-start | bytes 786440 | tf_op jit(solution)/shard_map/cond/branch_3_fun/ppermute | solution.py:43
  69.6 11.6 %collective-permute-start.111 = (bf16[128,1024]{1,0:T(8,128)(2,1)}, bf16[128,1024]{1,0:T(8,128)(2,1)}, u32[]{:S(2)}, u32[]{:S(2)}) collective-permute-start(bf16[128,1024]{1,0:T(8,128)(2,1)} %get-tuple-element.268), channel_id=1, source_target_pairs={{6,0},{7,1},{134,128},{135,129},{262,256},{263,257},{390,384},{391... | collective-permute-start | bytes 786440 | tf_op jit(solution)/shard_map/cond/branch_3_fun/ppermute | solution.py:43
  71.7 10.0 %collective-permute-start.113 = (bf16[128,1024]{1,0:T(8,128)(2,1)}, bf16[128,1024]{1,0:T(8,128)(2,1)}, u32[]{:S(2)}, u32[]{:S(2)}) collective-permute-start(bf16[128,1024]{1,0:T(8,128)(2,1)} %get-tuple-element.268), channel_id=1, source_target_pairs={{2,0},{3,1},{130,128},{131,129},{258,256},{259,257},{386,384},{387... | collective-permute-start | bytes 786440 | tf_op jit(solution)/shard_map/cond/branch_3_fun/ppermute | solution.py:43
  81.7 17.4 %collective-permute-start.115 = (bf16[1024,128]{1,0:T(8,128)(2,1)}, bf16[1024,128]{1,0:T(8,128)(2,1)S(1)}, u32[]{:S(2)}, u32[]{:S(2)}) collective-permute-start(bf16[1024,128]{1,0:T(8,128)(2,1)} %get-tuple-element.305.own_ref), channel_id=1, source_target_pairs={{1,0},{0,1},{129,128},{128,129},{257,256},{256,257},{385,384},{384... | collective-permute-start | bytes 786440 | tf_op jit(solution)/shard_map/ppermute | solution.py:43
  85.6 17.5 %collective-permute-start.116 = (bf16[128,1024]{1,0:T(8,128)(2,1)}, bf16[128,1024]{1,0:T(8,128)(2,1)S(1)}, u32[]{:S(2)}, u32[]{:S(2)}) collective-permute-start(bf16[128,1024]{1,0:T(8,128)(2,1)} %get-tuple-element.300.refs_2_), channel_id=1, source_target_pairs={{6,0},{7,1},{134,128},{135,129},{262,256},{263,257},{390,384},{391... | collective-permute-start | bytes 786440 | tf_op jit(solution)/shard_map/ppermute | solution.py:43
  88.8 14.4 %collective-permute-start.117 = (bf16[128,1024]{1,0:T(8,128)(2,1)}, bf16[128,1024]{1,0:T(8,128)(2,1)S(1)}, u32[]{:S(2)}, u32[]{:S(2)}) collective-permute-start(bf16[128,1024]{1,0:T(8,128)(2,1)} %get-tuple-element.303.refs_5_), channel_id=1, source_target_pairs={{2,0},{3,1},{130,128},{131,129},{258,256},{259,257},{386,384},{387... | collective-permute-start | bytes 786440 | tf_op jit(solution)/shard_map/ppermute | solution.py:43
  92.6 23.5 %collective-permute-start.119 = (bf16[128,1024]{1,0:T(8,128)(2,1)}, bf16[128,1024]{1,0:T(8,128)(2,1)S(1)}, u32[]{:S(2)}, u32[]{:S(2)}) collective-permute-start(bf16[128,1024]{1,0:T(8,128)(2,1)} %get-tuple-element.298.refs_0_), channel_id=1, source_target_pairs={{6,0},{7,1},{134,128},{135,129},{262,256},{263,257},{390,384},{391... | collective-permute-start | bytes 786440 | tf_op jit(solution)/shard_map/ppermute | solution.py:43
  94.5 23.5 %collective-permute-start.122 = (bf16[128,1024]{1,0:T(8,128)(2,1)}, bf16[128,1024]{1,0:T(8,128)(2,1)S(1)}, u32[]{:S(2)}, u32[]{:S(2)}) collective-permute-start(bf16[128,1024]{1,0:T(8,128)(2,1)} %get-tuple-element.299.refs_1_), channel_id=1, source_target_pairs={{2,0},{3,1},{130,128},{131,129},{258,256},{259,257},{386,384},{387... | collective-permute-start | bytes 786440 | tf_op jit(solution)/shard_map/ppermute | solution.py:43
  106.8 27.6 %collective-permute-start.118 = (bf16[256,1024]{1,0:T(8,128)(2,1)S(1)}, bf16[256,1024]{1,0:T(8,128)(2,1)S(1)}, u32[]{:S(2)}, u32[]{:S(2)}) collective-permute-start(bf16[256,1024]{1,0:T(8,128)(2,1)S(1)} %get-tuple-element.293), channel_id=1, source_target_pairs={{1,0},{0,1},{129,128},{128,129},{257,256},{256,257},{385,384},{384... | collective-permute-start | bytes 1572872 | tf_op jit(solution)/shard_map/ppermute | solution.py:43
  109.6 13.0 %collective-permute-start.120 = (bf16[128,1024]{1,0:T(8,128)(2,1)}, bf16[128,1024]{1,0:T(8,128)(2,1)S(1)}, u32[]{:S(2)}, u32[]{:S(2)}) collective-permute-start(bf16[128,1024]{1,0:T(8,128)(2,1)} %get-tuple-element.299.refs_1_), channel_id=1, source_target_pairs={{6,0},{7,1},{134,128},{135,129},{262,256},{263,257},{390,384},{391... | collective-permute-start | bytes 786440 | tf_op jit(solution)/shard_map/ppermute | solution.py:43
  111.5 11.1 %collective-permute-start.121 = (bf16[128,1024]{1,0:T(8,128)(2,1)}, bf16[128,1024]{1,0:T(8,128)(2,1)S(1)}, u32[]{:S(2)}, u32[]{:S(2)}) collective-permute-start(bf16[128,1024]{1,0:T(8,128)(2,1)} %get-tuple-element.298.refs_0_), channel_id=1, source_target_pairs={{2,0},{3,1},{130,128},{131,129},{258,256},{259,257},{386,384},{387... | collective-permute-start | bytes 786440 | tf_op jit(solution)/shard_map/ppermute | solution.py:43
  116.1 10.4 %collective-permute-start.123 = (bf16[128,1024]{1,0:T(8,128)(2,1)S(1)}, bf16[128,1024]{1,0:T(8,128)(2,1)S(1)}, u32[]{:S(2)}, u32[]{:S(2)}) collective-permute-start(bf16[128,1024]{1,0:T(8,128)(2,1)S(1)} %collective-permute-done.119.refs_2_), channel_id=1, source_target_pairs={{6,0},{7,1},{134,128},{135,129},{262,256},{263,257},{390,384},{391... | collective-permute-start | bytes 786440 | tf_op jit(solution)/shard_map/ppermute | solution.py:43
  118.0 9.3 %collective-permute-start.124 = (bf16[128,1024]{1,0:T(8,128)(2,1)S(1)}, bf16[128,1024]{1,0:T(8,128)(2,1)S(1)}, u32[]{:S(2)}, u32[]{:S(2)}) collective-permute-start(bf16[128,1024]{1,0:T(8,128)(2,1)S(1)} %collective-permute-done.122.refs_5_), channel_id=1, source_target_pairs={{2,0},{3,1},{130,128},{131,129},{258,256},{259,257},{386,384},{387... | collective-permute-start | bytes 786440 | tf_op jit(solution)/shard_map/ppermute | solution.py:43
  130.7 5.2 %collective-permute-start.125 = (bf16[256,1024]{1,0:T(8,128)(2,1)S(1)}, bf16[256,1024]{1,0:T(8,128)(2,1)S(1)}, u32[]{:S(2)}, u32[]{:S(2)}) collective-permute-start(bf16[256,1024]{1,0:T(8,128)(2,1)S(1)} %get-tuple-element.297), channel_id=1, source_target_pairs={{1,0},{0,1},{129,128},{128,129},{257,256},{256,257},{385,384},{384... | collective-permute-start | bytes 1572872 | tf_op jit(solution)/shard_map/ppermute | solution.py:43
where the time goes:
time: 139 us; the launch traced here: 138 us
  starting transfers between devices  89.9 us (65%)
  waiting for transfers between devices  28.7 us (21%)
  Pallas kernels  10.9 us (8%)
  local copies, waits for them, and re-layouts  4.18 us (3%)
  other arithmetic  1.89 us (1%)
  between operations  1.84 us (1%)
    ppermute x21, starting transfers between devices, moved(): return lax.ppermute(block, AXES, route(source_of))  75.1 us
    ppermute x21, waiting for transfers between devices, moved(): return lax.ppermute(block, AXES, route(source_of))  28.7 us
    all_to_all x1, starting transfers between devices, third_stage(): own = lax.all_to_all(slab, 'grid', split_axis=1, concat_axis=0, tiled=True)  14.8 us
    pallas_call x2, Pallas kernels, product(): pl.pallas_call(product_kernel, grid=(columns // tile,), out_shape=[jax.Sh...  7.05 us
    pallas_call x1, Pallas kernels, left_operators(): pl.pallas_call(left_kernel, out_shape=jax.ShapeDtypeStruct((2, SLABS, 2 *...  3.82 us
  transfers between devices with their start and end apart: 22, of which 7 were waited for; matrix products, arithmetic and copies ran while one was open for 2% of the time, Pallas kernels for 8%

commit v1 on v0

v1 whole, which is shorter than its diff:
```python
import functools
import math

import jax
import jax.numpy as jnp
from jax import lax
from jax.experimental import pallas as pl
from jax.experimental.pallas import tpu as pltpu
from jax.sharding import PartitionSpec as P

SIDE = 16
DEPTH = 96
TWO_PI = 2.0 * math.pi

Z_LO, Y, Z_HI, X, CORE = 4, 8, 2, 4, 2
Z = Z_LO * Z_HI
POINTS = Z_LO * Y
AXES = ("ka", "grid")
SLABS = 16
SLAB_ROWS = 32
PER_ATOM = 8
HIGHEST = lax.Precision.HIGHEST


def flat_id(x, y, z, core):
    return (((z % Z_LO) * Y + y) * Z_HI + z // Z_LO) * (X * CORE) + x * CORE + core


def route(source_of):
    pairs = []
    for x in range(X):
        for y in range(Y):
            for z in range(Z):
                for core in range(CORE):
                    source = source_of(x, y, z, core)
                    if source is None:
                        continue
                    sx, sy, sz, sc = source
                    pairs.append(
                        (flat_id(sx % X, sy % Y, sz % Z, sc), flat_id(x, y, z, core))
                    )
    return pairs


def moved(block, source_of):
    return lax.ppermute(block, AXES, route(source_of))


def from_other_core(block):
    return moved(block, lambda x, y, z, core: (x, y, z, 1 - core))


def from_x(block, offset):
    return moved(block, lambda x, y, z, core: (x + offset, y, z, core))


def z_offset(distance, core, y):
    part = (distance // Y + 2 + (y + distance % Y) // Y) % Z_LO
    other_way = (part == 2) * core * (distance % Y != 0)
    return part - Z_LO * (part == 3) - Z_LO * other_way


class Place:
    def __init__(self, partner):
        point, member = lax.axis_index("ka"), lax.axis_index("grid")
        self.core = member & (CORE - 1)
        self.x = (member >> 1) & (X - 1)
        self.z_hi = member >> 3
        self.y = point & (Y - 1)
        self.z = self.z_hi * Z_LO + (point >> 3)
        distances = [(partner[0, v] - point) & (POINTS - 1) for v in range(2)]
        along = [d & (Y - 1) for d in distances]
        hops = [jnp.minimum(d, Y - d) for d in along]
        swapped = hops[0] > hops[1]
        self.swap = jnp.where(swapped, 1, 0)
        self.distances = [
            jnp.where(swapped, distances[1 - v], distances[v]) for v in range(2)
        ]

    def first_hi(self, v):
        distance = self.distances[v]
        along = distance & (Y - 1)
        part = ((distance >> 3) + 2 + ((self.y + along) >> 3)) & (Z_LO - 1)
        other_way = (part == 2) & (self.core == 1) & (along != 0)
        back = jnp.where((part == 3) | other_way, Z_LO, 0)
        return ((self.z - 2 + part - back) & (Z - 1)) >> 2


def from_other_half(block):
    return moved(
        block,
        lambda x, y, z, core: None if core == z // Z_LO else (x, y, z + Z_LO, 1 - core),
    )


def toward_partner(lane, distance):
    def source(x, y, z, core):
        return x, (y + distance) % Y, z + z_offset(distance, core, y), core

    if all(source(0, y, 0, c) == (0, y, 0, c) for y in range(Y) for c in range(CORE)):
        return lane
    return moved(lane, source)


def both_halves(lane):
    behind = moved(lane, lambda x, y, z, core: (x, y, z - 2, core))
    ahead = moved(lane, lambda x, y, z, core: (x, y, z + 2, core))
    return behind, ahead


def dot00(left, right, precision=None):
    return lax.dot_general(
        left,
        right,
        (((0,), (0,)), ((), ())),
        precision=precision,
        preferred_element_type=jnp.float32,
    )


def left_kernel(
    partner_ref,
    b_ref,
    shift_ref,
    own_ref,
    other_ref,
    proj_ref,
    support_ref,
    counts_ref,
    aug_ref,
    sites_ref,
    out_ref,
    real_ref,
    imag_ref,
    masked_ref,
    both_ref,
):
    atoms = support_ref.shape[1]
    nproj = proj_ref.shape[1]
    rows = proj_ref.shape[0]
    width = own_ref.shape[2] // 2
    place = Place(partner_ref)
    core = place.core
    f32 = jnp.float32

    atom_of = lax.broadcasted_iota(jnp.int32, (atoms, nproj), 1) // PER_ATOM
    spread = (atom_of == lax.broadcasted_iota(jnp.int32, (atoms, nproj), 0)).astype(f32)
    reach = jnp.dot(support_ref[...].astype(f32), spread, preferred_element_type=f32)
    counts = jnp.broadcast_to(counts_ref[...].astype(f32), (8, atoms))
    counts = jnp.dot(counts, spread, preferred_element_type=f32)[0:1]
    slot_id = (lax.broadcasted_iota(jnp.int32, (1, nproj), 1) % PER_ATOM).astype(f32)
    keep = reach * (slot_id < counts - 0.5).astype(f32)
    both_ref[core] = own_ref[...]
    both_ref[1 - core] = other_ref[...]
    for s in range(SLABS):
        at = pl.ds(s * SLAB_ROWS, SLAB_ROWS)
        masked_ref[at, :] = (proj_ref[at, :].astype(f32) * keep[s : s + 1, :]).astype(
            jnp.bfloat16
        )
        slab_hi, slab_x, slab_core = s // (CORE * X), s // CORE % X, s % CORE
        slab = CORE * ((place.x - slab_x) & (X - 1)) + (slab_core ^ place.z_hi)
        for side in range(2):
            lanes = pl.ds(pl.multiple_of((core ^ side) * width, width), width)
            to = pl.ds(side * width, width)
            real_ref[at, to] = both_ref[slab_hi, slab, pl.ds(0, SLAB_ROWS), lanes]
            imag_ref[at, to] = both_ref[slab_hi, slab, pl.ds(SLAB_ROWS, SLAB_ROWS), lanes]

    masked = masked_ref[...]
    proj_real = dot00(masked, real_ref[...]).astype(jnp.bfloat16).astype(f32)
    proj_imag = dot00(masked, imag_ref[...]).astype(jnp.bfloat16).astype(f32)

    by_pair = jnp.dot(aug_ref[...], spread, precision=HIGHEST, preferred_element_type=f32)
    column = lax.broadcasted_iota(jnp.int32, (PER_ATOM, nproj), 1) % PER_ATOM
    pick = column == lax.broadcasted_iota(jnp.int32, (PER_ATOM, nproj), 0)
    by_row = [
        jnp.sum(
            jnp.where(pick, by_pair[i * PER_ATOM : (i + 1) * PER_ATOM], 0.0),
            axis=0,
            keepdims=True,
        )
        for i in range(PER_ATOM)
    ]
    tiled = jnp.concatenate(by_row * atoms, axis=0)
    same_atom = (
        lax.broadcasted_iota(jnp.int32, (nproj, nproj), 0) // PER_ATOM
        == lax.broadcasted_iota(jnp.int32, (nproj, nproj), 1) // PER_ATOM
    )
    aug = jnp.where(same_atom, tiled, 0.0)
    aug_real = dot00(aug, proj_real, HIGHEST)
    aug_imag = dot00(aug, proj_imag, HIGHEST)

    sites = jnp.dot(sites_ref[...], spread, precision=HIGHEST, preferred_element_type=f32)
    chunks = rows // 128
    lanes = lax.broadcasted_iota(jnp.int32, (8, 128), 1)
    block = lax.broadcasted_iota(jnp.int32, (8, 128), 0)
    row_ids = block * 128 + lanes
    along_a = (row_ids % SIDE).astype(f32) / SIDE
    along_b = (row_ids // SIDE % SIDE).astype(f32) / SIDE
    along_c = (row_ids // (SIDE * SIDE)).astype(f32) / DEPTH

    for v in range(2):
        vector = v ^ place.swap
        first_hi = place.first_hi(v)
        q = [
            b_ref[vector, axis] + shift_ref[0, vector, axis].astype(f32)
            for axis in range(3)
        ]
        theta = TWO_PI * (q[0] * along_a + q[1] * along_b + q[2] * along_c)
        phi = TWO_PI * (q[0] * sites[0:1] + q[1] * sites[1:2] + q[2] * sites[2:3])
        angle = theta
        for part in range(nproj // 128):
            piece = phi[0:1, part * 128 : (part + 1) * 128]
            angle = jnp.where(block == chunks + part, piece, angle)
        cosine = jnp.transpose(jnp.cos(angle))
        sine = jnp.transpose(jnp.sin(angle))
        weights = []
        for part in range(nproj // 128):
            at = slice(part * 128, (part + 1) * 128)
            cos_p = cosine[:, chunks + part : chunks + part + 1]
            sin_p = sine[:, chunks + part : chunks + part + 1]
            weights.append(
                (
                    cos_p * aug_real[at] - sin_p * aug_imag[at],
                    cos_p * aug_imag[at] + sin_p * aug_real[at],
                )
            )
        weight_real = jnp.concatenate([w[0] for w in weights], axis=0)
        weight_imag = jnp.concatenate([w[1] for w in weights], axis=0)

        def spread_rows(weight):
            high = weight.astype(jnp.bfloat16)
            low = (weight - high.astype(f32)).astype(jnp.bfloat16)
            return jnp.dot(masked, high, preferred_element_type=f32) + jnp.dot(
                masked, low, preferred_element_type=f32
            )

        added_real = spread_rows(weight_real)
        added_imag = spread_rows(weight_imag)
        per_chunk = 128 // SLAB_ROWS
        for s in range(SLABS):
            chunk, inside = s // per_chunk, s % per_chunk * SLAB_ROWS
            at = slice(s * SLAB_ROWS, (s + 1) * SLAB_ROWS)
            cos_r = cosine[inside : inside + SLAB_ROWS, chunk : chunk + 1]
            sin_r = sine[inside : inside + SLAB_ROWS, chunk : chunk + 1]
            wave_real = real_ref[at, :].astype(f32)
            wave_imag = imag_ref[at, :].astype(f32)
            left_real = cos_r * wave_real - sin_r * wave_imag + added_real[at]
            left_imag = cos_r * wave_imag + sin_r * wave_real + added_imag[at]
            left_real = left_real.astype(jnp.bfloat16)
            left_imag = left_imag.astype(jnp.bfloat16)
            slab_hi, slab_x, slab_core = s // (CORE * X), s // CORE % X, s % CORE
            step = (slab_x - place.x) & (X - 1)
            piece = jnp.where(step == 3, 1, jnp.where(step == 0, 0, step + 1))
            slot = piece * 4 + (slab_hi ^ first_hi) * 2 + (slab_core ^ core)
            top, low = pl.ds(0, SLAB_ROWS), pl.ds(SLAB_ROWS, SLAB_ROWS)
            for side in range(2):
                real_half = left_real[:, side * width : (side + 1) * width]
                imag_half = left_imag[:, side * width : (side + 1) * width]
                base = side * 2 * width
                out_ref[v, slot, top, base : base + width] = real_half
                out_ref[v, slot, low, base : base + width] = imag_half
                out_ref[v, slot, top, base + width : base + 2 * width] = -imag_half
                out_ref[v, slot, low, base + width : base + 2 * width] = real_half


def left_operators(partner, b_vectors, shift, own, other, projectors, support, counts, aug, sites):
    rows, nproj = projectors.shape
    width = own.shape[2] // 2
    smem = pl.BlockSpec(memory_space=pltpu.SMEM)
    vmem = pl.BlockSpec(memory_space=pltpu.VMEM)
    return pl.pallas_call(
        left_kernel,
        out_shape=jax.ShapeDtypeStruct((2, SLABS, 2 * SLAB_ROWS, 4 * width), jnp.bfloat16),
        in_specs=[smem] * 3 + [vmem] * 7,
        out_specs=vmem,
        scratch_shapes=[
            pltpu.VMEM((rows, 2 * width), jnp.bfloat16),
            pltpu.VMEM((rows, 2 * width), jnp.bfloat16),
            pltpu.VMEM((rows, nproj), jnp.bfloat16),
            pltpu.VMEM((2,) + own.shape, jnp.bfloat16),
        ],
        compiler_params=pltpu.CompilerParams(vmem_limit_bytes=28 * 1024 * 1024),
        cost_estimate=pl.CostEstimate(
            flops=2_000_000_000, bytes_accessed=4 * 1024 * 1024, transcendentals=4096
        ),
        name="left_operators",
    )(partner, b_vectors, shift, own, other, projectors, support, counts, aug, sites)


def product_kernel(partner_ref, left_ref, held, from_left, from_right, far_left, far_right, out_ref):
    swap = Place(partner_ref).swap
    rows = held.shape[0] // 4
    for v in range(2):
        near, far = pl.ds(v * rows, rows), pl.ds((2 + v) * rows, rows)
        pieces = [ref[at, :] for ref in (held, from_left, from_right) for at in (near, far)]
        pieces = pieces + [far_left[near, :], far_right[near, :]]
        right = jnp.concatenate(pieces, axis=0)
        out_ref[v ^ swap] = dot00(left_ref[v], right).astype(jnp.bfloat16)


def products(partner, left, side, pieces):
    depth = left.shape[1]
    half = left.shape[2] // 2
    columns = pieces[0].shape[1]
    return pl.pallas_call(
        product_kernel,
        grid=(1,),
        out_shape=jax.ShapeDtypeStruct((2, half, columns), jnp.bfloat16),
        in_specs=[
            pl.BlockSpec(memory_space=pltpu.SMEM),
            pl.BlockSpec((2, depth, half), lambda i: (0, 0, side)),
        ]
        + [pl.BlockSpec(piece.shape, lambda i: (0, 0)) for piece in pieces],
        out_specs=pl.BlockSpec((2, half, columns), lambda i: (0, 0, 0)),
        compiler_params=pltpu.CompilerParams(vmem_limit_bytes=28 * 1024 * 1024),
        cost_estimate=pl.CostEstimate(
            flops=4 * depth * half * columns,
            bytes_accessed=7 * 1024 * 1024,
            transcendentals=0,
        ),
        name="products",
    )(partner, left, *pieces)


def body(
    wavefunctions,
    projectors,
    support,
    proj_counts,
    aug_matrices,
    atom_sites,
    b_vectors,
    partner,
    lattice_shift,
):
    waves = wavefunctions[0]
    row_count, _, bands = waves.shape
    half_bands = bands // CORE
    place = Place(partner)
    core, x, z_hi, distances = place.core, place.x, place.z_hi, place.distances

    slab = jnp.transpose(waves, (1, 0, 2)).reshape(2 * row_count, bands)
    low, high = slab[:, :half_bands], slab[:, half_bands:]
    kept = jnp.where(core == 0, low, high)
    given = jnp.where(core == 0, high, low)
    lane = jnp.concatenate([kept, from_other_core(given)], axis=0)
    half_rows = lane.shape[0]

    chip_bands = half_bands // X

    def bands_of(lane, offset):
        start = (x + offset) % X * chip_bands
        return lax.dynamic_slice_in_dim(lane, start, chip_bands, axis=1)

    def first_stage(distance, lane):
        onward = jnp.concatenate([bands_of(lane, 1), bands_of(lane, 2)], axis=0)
        return (
            toward_partner(lane, distance),
            from_x(onward, -1),
            from_x(bands_of(lane, -1), 1),
        )

    def second_stage(distance, lane, moved_first, onward):
        held_first = both_halves(moved_first)
        return (
            toward_partner(lane, distance),
            held_first,
            from_x(onward[half_rows:], -1),
        )

    moved_first, one_back, one_on = lax.switch(
        distances[0],
        [functools.partial(first_stage, d) for d in range(POINTS)],
        lane,
    )
    moved_second, held_first, two_back = lax.switch(
        distances[1],
        [functools.partial(second_stage, d) for d in range(POINTS)],
        lane,
        moved_first,
        one_back,
    )
    held_second = both_halves(moved_second)
    held = jnp.concatenate(
        [held_first[0], held_second[0], held_first[1], held_second[1]], axis=0
    )
    from_left, from_right = from_x(held, -1), from_x(held, 1)
    far_left = from_x(from_left[: 2 * half_rows], -1)
    far_right = from_x(from_right[2 * half_rows :], 1)
    own = jnp.concatenate([bands_of(lane, 0), one_back[:half_rows], two_back, one_on], axis=0)
    own = jnp.where(core == z_hi, own, from_other_half(own))
    other = from_other_core(own)
    own_shape = (X * CORE, 2 * row_count, chip_bands)
    own, other = own.reshape(own_shape), other.reshape(own_shape)
    left = left_operators(
        partner,
        b_vectors,
        lattice_shift,
        own,
        other,
        projectors,
        jnp.transpose(support),
        proj_counts.reshape(1, -1),
        jnp.transpose(aug_matrices, (1, 2, 0)).reshape(-1, support.shape[0]),
        jnp.transpose(atom_sites),
    )
    left = left.reshape(2, left.shape[1] * left.shape[2], left.shape[3])

    pieces = (held, from_left, from_right, far_left, far_right)
    theirs = products(partner, left, 1, pieces)
    got = from_other_core(theirs)
    mine = products(partner, left, 0, pieces)
    final = jnp.concatenate(
        [jnp.where(core == 0, mine, got), jnp.where(core == 0, got, mine)], axis=2
    )
    return final.reshape(1, 2, 2, bands // SLABS, bands)


def solution(mesh):
    in_specs = (
        P("ka", "grid", None, None),
        P(),
        P(),
        P(),
        P(),
        P(),
        P(),
        P("ka", None),
        P("ka", None, None),
    )
    out_specs = P("ka", None, None, "grid", None)
    return jax.shard_map(body, mesh=mesh, in_specs=in_specs, out_specs=out_specs, check_vma=False)
```

time: 139 us -> 128 us (0.921)
  starting transfers between devices: 89.9 us -> 64.8 us
  waiting for transfers between devices: 28.7 us -> 41.3 us
  Pallas kernels: 10.9 us -> 6.63 us
  local copies, waits for them, and re-layouts: 4.18 us -> 7.53 us
  other arithmetic: 1.89 us -> 5.15 us
    all_to_all x1 -> x0, starting transfers between devices: 14.8 us -> none  [third_stage(): own = lax.all_to_all(slab, 'grid', split_axis=1, concat_axis=0, tiled=True)]
    ppermute x21 -> x16, waiting for transfers between devices: 28.7 us -> 41.3 us  [moved(): return lax.ppermute(block, AXES, route(source_of))]
    ppermute x21 -> x16, starting transfers between devices: 75.1 us -> 64.8 us  [moved(): return lax.ppermute(block, AXES, route(source_of))]
    pallas_call x2, Pallas kernels: 7.05 us -> 3.65 us  [products(): pl.pallas_call(product_kernel, grid=(1,), out_shape=jax.ShapeDtypeStruct(...]
    concatenate x2 -> x3, other arithmetic: 0.16 us -> 3.14 us  [the longest x1 1.62 us: body(): jnp.concatenate([bands_of(lane, 0), one_back[:half_rows], two_back, one_o...]
    unnamed x15 -> x27, local copies, waits for them, and re-layouts: 0.11 us -> 2.64 us
    slice x2 -> x5, local copies, waits for them, and re-layouts: 1.44 us -> 3.1 us  [the longest x1 1.33 us: __init__(): distances = [partner[0, v] - point & POINTS - 1 for v in range(2)]]
    another operation x2 -> x0, other arithmetic: 1.51 us -> none  [the longest x1 1.5 us: body(): jnp.stack([joined(mine_first, got_first), joined(mine_second, got_second)])]
  transfers between devices with their start and end apart: 22 -> 16, of which waited for: 7 -> 10; matrix products, arithmetic and copies ran while one was open for 2% -> 7% of each run, Pallas kernels for 8% -> 4%
where the time goes in v1:
time: 128 us; the launch traced here: 127 us
  starting transfers between devices  64.8 us (51%)
  waiting for transfers between devices  41.3 us (32%)
  local copies, waits for them, and re-layouts  7.53 us (6%)
  Pallas kernels  6.63 us (5%)
  other arithmetic  5.15 us (4%)
  between operations  1.7 us (1%)
    ppermute x16, starting transfers between devices, moved(): return lax.ppermute(block, AXES, route(source_of))  64.8 us
    ppermute x16, waiting for transfers between devices, moved(): return lax.ppermute(block, AXES, route(source_of))  41.3 us
    pallas_call x2, Pallas kernels, products(): pl.pallas_call(product_kernel, grid=(1,), out_shape=jax.ShapeDtypeStruct(...  3.65 us
    pallas_call x1, Pallas kernels, left_operators(): pl.pallas_call(left_kernel, out_shape=jax.ShapeDtypeStruct((2, SLABS, 2 *...  2.98 us
    unnamed x27, local copies, waits for them, and re-layouts  2.64 us
  transfers between devices with their start and end apart: 16, of which 10 were waited for; matrix products, arithmetic and copies ran while one was open for 7% of the time, Pallas kernels for 4%

profile of v1, /device:TPU:1, one launch (start us, length us, event | category | flops | bytes accessed | tf_op | source)
XLA Modules:
  0.0 127.4 jit_solution(14595098766399679401)
XLA Ops:
  0.0 1.0 copy.10
  1.1 0.0 copy-start.8
  1.1 8.8 %collective-permute-start.222 = (bf16[64,1024]{1,0:T(8,128)(2,1)S(1)}, bf16[64,1024]{1,0:T(8,128)(2,1)S(1)}, u32[]{:S(2)}, u32[]{:S(2)}) collective-permute-start(bf16[64,1024]{1,0:T(8,128)(2,1)S(1)} %get-tuple-element.601), channel_id=1, source_target_pairs={{1,0},{0,1},{129,128},{128,129},{257,256},{256,257},{385,384},{384... | collective-permute-start | bytes 393224 | tf_op jit(solution)/shard_map/ppermute | solution.py:46
  9.9 1.3 %fusion.1 = (s32[1,1]{1,0:T(1,128)}, s32[1,1]{1,0:T(1,128)}) fusion(s32[1,2]{1,0:T(1,128)} %partner_ref.5), kind=kLoop, calls=%fused_computation.143 | loop fusion | bytes 16 | tf_op jit(solution)/shard_map/slice | solution.py:71
  12.6 0.6 copy-done.11
  13.2 9.2 %conditional.2 = (bf16[128,1024]{1,0:T(8,128)(2,1)}, bf16[256,256]{1,0:T(8,128)(2,1)}, bf16[128,256]{1,0:T(8,128)(2,1)}, bf16[128,256]{1,0:T(8,128)(2,1)S(1)}) conditional(s32[]{:T(128)} %clamp.6, (bf16[128,1024]{1,0:T(8,128)(2,1)S(1)}, s32[]{:T(128)}) %tuple.293, (bf16[128,1024]{1,0:T(8,128)(2,1)S(1)}, ...), branch_computations={%region_0.1_spmd, %region_1.2_spmd, %region_2.3_spmd, %region_3.4_... | conditional | flops 262192 | bytes 2622105 | solution.py:371
  13.3 1.9 %collective-permute-start.175 = (bf16[256,256]{1,0:T(8,128)(2,1)S(1)}, bf16[256,256]{1,0:T(8,128)(2,1)}, u32[]{:S(2)}, u32[]{:S(2)}) collective-permute-start(bf16[256,256]{1,0:T(8,128)(2,1)S(1)} %pad_maximum_fusion.16), channel_id=1, source_target_pairs={{6,0},{7,1},{134,128},{135,129},{262,256},{263,257},{390,384},{391... | collective-permute-start | bytes 393224 | tf_op jit(solution)/shard_map/cond/branch_16_fun/ppermute | solution.py:46
  15.2 4.6 %collective-permute-start.176 = (bf16[128,256]{1,0:T(8,128)(2,1)S(1)}, bf16[128,256]{1,0:T(8,128)(2,1)}, u32[]{:S(2)}, u32[]{:S(2)}) collective-permute-start(bf16[128,256]{1,0:T(8,128)(2,1)S(1)} %get-tuple-element.550), channel_id=1, source_target_pairs={{2,0},{3,1},{130,128},{131,129},{258,256},{259,257},{386,384},{387... | collective-permute-start | bytes 196616 | tf_op jit(solution)/shard_map/cond/branch_16_fun/ppermute | solution.py:46
  19.8 0.7 copy.75
  20.5 1.1 collective-permute-done.175
  21.6 0.8 slice.233
  22.5 23.9 %conditional.3 = (bf16[128,1024]{1,0:T(8,128)(2,1)}, bf16[128,1024]{1,0:T(8,128)(2,1)}, bf16[128,1024]{1,0:T(8,128)(2,1)}, bf16[128,256]{1,0:T(8,128)(2,1)}) conditional(s32[]{:T(128)} %clamp.7, (bf16[128,1024]{1,0:T(8,128)(2,1)S(1)}, bf16[128,1024]{1,0:T(8,128)(2,1)}, bf16[256,256]{1,0:T(8,128)(2,1)}) %tuple.295, ...), branch_computations={%region_32.33_spmd, %region_33.34_spmd, %region_34.35_spmd, %regio... | conditional | bytes 3539136 | solution.py:376
  22.7 4.9 %collective-permute-start.107 = (bf16[128,1024]{1,0:T(8,128)(2,1)S(1)}, bf16[128,1024]{1,0:T(8,128)(2,1)}, u32[]{:S(2)}, u32[]{:S(2)}) collective-permute-start(bf16[128,1024]{1,0:T(8,128)(2,1)S(1)} %get-tuple-element.471), channel_id=1, source_target_pairs={{176,0},{177,1},{304,128},{305,129},{432,256},{433,257},{56,384},{... | collective-permute-start | bytes 786440 | tf_op jit(solution)/shard_map/cond/branch_27_fun/ppermute | solution.py:46
  27.7 2.3 %collective-permute-start.109 = (bf16[128,1024]{1,0:T(8,128)(2,1)}, bf16[128,1024]{1,0:T(8,128)(2,1)}, u32[]{:S(2)}, u32[]{:S(2)}) collective-permute-start(bf16[128,1024]{1,0:T(8,128)(2,1)} %get-tuple-element.472), channel_id=1, source_target_pairs={{256,0},{257,1},{384,128},{385,129},{8,256},{9,257},{136,384},{137... | collective-permute-start | bytes 786440 | tf_op jit(solution)/shard_map/cond/branch_27_fun/ppermute | solution.py:46
  30.0 6.6 %collective-permute-start.108 = (bf16[128,1024]{1,0:T(8,128)(2,1)}, bf16[128,1024]{1,0:T(8,128)(2,1)}, u32[]{:S(2)}, u32[]{:S(2)}) collective-permute-start(bf16[128,1024]{1,0:T(8,128)(2,1)} %get-tuple-element.472), channel_id=1, source_target_pairs={{264,0},{265,1},{392,128},{393,129},{0,256},{1,257},{128,384},{129... | collective-permute-start | bytes 786440 | tf_op jit(solution)/shard_map/cond/branch_27_fun/ppermute | solution.py:46
  36.6 0.8 slice.200
  37.5 1.9 %collective-permute-start.110 = (bf16[128,256]{1,0:T(8,128)(2,1)S(1)}, bf16[128,256]{1,0:T(8,128)(2,1)}, u32[]{:S(2)}, u32[]{:S(2)}) collective-permute-start(bf16[128,256]{1,0:T(8,128)(2,1)S(1)} %slice.200), channel_id=1, source_target_pairs={{6,0},{7,1},{134,128},{135,129},{262,256},{263,257},{390,384},{391... | collective-permute-start | bytes 196616 | tf_op jit(solution)/shard_map/cond/branch_27_fun/ppermute | solution.py:46
  39.4 4.7 %collective-permute-done.110 = bf16[128,256]{1,0:T(8,128)(2,1)} collective-permute-done((bf16[128,256]{1,0:T(8,128)(2,1)S(1)}, bf16[128,256]{1,0:T(8,128)(2,1)}, u32[]{:S(2)}, u32[]{:S(2)}) %collective-permute-start.110) | collective-permute-done | bytes 65568 | tf_op jit(solution)/shard_map/cond/branch_27_fun/ppermute | solution.py:46
  44.1 1.6 %collective-permute-done.107 = bf16[128,1024]{1,0:T(8,128)(2,1)} collective-permute-done((bf16[128,1024]{1,0:T(8,128)(2,1)S(1)}, bf16[128,1024]{1,0:T(8,128)(2,1)}, u32[]{:S(2)}, u32[]{:S(2)}) %collective-permute-start.107) | collective-permute-done | bytes 262176 | tf_op jit(solution)/shard_map/cond/branch_27_fun/ppermute | solution.py:46
  45.7 0.7 collective-permute-done.109
  46.3 7.6 %collective-permute-start.225 = (bf16[128,1024]{1,0:T(8,128)(2,1)}, bf16[128,1024]{1,0:T(8,128)(2,1)S(1)}, u32[]{:S(2)}, u32[]{:S(2)}) collective-permute-start(bf16[128,1024]{1,0:T(8,128)(2,1)} %get-tuple-element.500), channel_id=1, source_target_pairs={{264,0},{265,1},{392,128},{393,129},{0,256},{1,257},{128,384},{129... | collective-permute-start | bytes 786440 | tf_op jit(solution)/shard_map/ppermute | solution.py:46
  54.0 1.9 %collective-permute-start.226 = (bf16[128,1024]{1,0:T(8,128)(2,1)}, bf16[128,1024]{1,0:T(8,128)(2,1)S(1)}, u32[]{:S(2)}, u32[]{:S(2)}) collective-permute-start(bf16[128,1024]{1,0:T(8,128)(2,1)} %get-tuple-element.500), channel_id=1, source_target_pairs={{256,0},{257,1},{384,128},{385,129},{8,256},{9,257},{136,384},{137... | collective-permute-start | bytes 786440 | tf_op jit(solution)/shard_map/ppermute | solution.py:46
  55.9 1.0 constant_dynamic-update-slice_fusion.3
  56.9 4.2 %collective-permute-done.225 = bf16[128,1024]{1,0:T(8,128)(2,1)S(1)} collective-permute-done((bf16[128,1024]{1,0:T(8,128)(2,1)}, bf16[128,1024]{1,0:T(8,128)(2,1)S(1)}, u32[]{:S(2)}, u32[]{:S(2)}) %collective-permute-start.225) | collective-permute-done | bytes 262176 | tf_op jit(solution)/shard_map/ppermute | solution.py:46
  61.1 1.0 constant_dynamic-update-slice_fusion.1
  62.1 0.0 copy-start
  62.1 0.0 copy-start.1
  62.1 0.0 copy-start.4
  62.2 10.4 %collective-permute-done.226 = bf16[128,1024]{1,0:T(8,128)(2,1)S(1)} collective-permute-done((bf16[128,1024]{1,0:T(8,128)(2,1)}, bf16[128,1024]{1,0:T(8,128)(2,1)S(1)}, u32[]{:S(2)}, u32[]{:S(2)}) %collective-permute-start.226) | collective-permute-done | bytes 262176 | tf_op jit(solution)/shard_map/ppermute | solution.py:46
  72.6 1.9 %collective-permute-start.228 = (bf16[512,1024]{1,0:T(8,128)(2,1)S(1)}, bf16[512,1024]{1,0:T(8,128)(2,1)S(1)}, u32[]{:S(2)}, u32[]{:S(2)}) collective-permute-start(bf16[512,1024]{1,0:T(8,128)(2,1)S(1)} %constant_dynamic-update-slice_fusion.held), channel_id=1, source_target_pairs={{2,0},{3,1},{130,128},{131,129},{258,256},{259,257},{386,384},{387... | collective-permute-start | bytes 3145736 | tf_op jit(solution)/shard_map/ppermute | solution.py:46
  74.5 3.4 %collective-permute-start.227 = (bf16[512,1024]{1,0:T(8,128)(2,1)S(1)}, bf16[512,1024]{1,0:T(8,128)(2,1)S(1)}, u32[]{:S(2)}, u32[]{:S(2)}) collective-permute-start(bf16[512,1024]{1,0:T(8,128)(2,1)S(1)} %constant_dynamic-update-slice_fusion.held), channel_id=1, source_target_pairs={{6,0},{7,1},{134,128},{135,129},{262,256},{263,257},{390,384},{391... | collective-permute-start | bytes 3145736 | tf_op jit(solution)/shard_map/ppermute | solution.py:46
  77.9 0.8 fusion
  78.7 1.6 %pad_maximum_fusion.34 = bf16[512,256]{1,0:T(8,128)(2,1)} fusion(bf16[128,256]{1,0:T(8,128)(2,1)} %get-tuple-element.498, bf16[128,256]{1,0:T(8,128)(2,1)} %get-tuple-element.497, bf16[128,256]{1,0:T(8,128)(2,1)} %copy-done.9, bf16[128,256]{1,0:T(8,128)(2,1)S(1)} %fusion), kind=kLoop, calls=%fused_computation.134 | loop fusion | flops 1048576 | bytes 524288 | tf_op jit(solution)/shard_map/concatenate | solution.py:390
  80.3 5.7 %collective-permute-start.223 = (bf16[512,256]{1,0:T(8,128)(2,1)}, bf16[512,256]{1,0:T(8,128)(2,1)}, u32[]{:S(2)}, u32[]{:S(2)}) collective-permute-start(bf16[512,256]{1,0:T(8,128)(2,1)} %pad_maximum_fusion.34), channel_id=1, source_target_pairs={{8,1},{136,129},{264,257},{392,385},{1,8},{129,136},{257,264},{385... | collective-permute-start | bytes 786440 | tf_op jit(solution)/shard_map/ppermute | solution.py:46
  86.1 12.7 %collective-permute-done.228.from_right = bf16[512,1024]{1,0:T(8,128)(2,1)S(1)} collective-permute-done((bf16[512,1024]{1,0:T(8,128)(2,1)S(1)}, bf16[512,1024]{1,0:T(8,128)(2,1)S(1)}, u32[]{:S(2)}, u32[]{:S(2)}) %collective-permute-start.228) | collective-permute-done | bytes 1048608 | tf_op jit(solution)/shard_map/ppermute | solution.py:46
  98.8 3.4 %collective-permute-start.230 = (bf16[256,1024]{1,0:T(8,128)(2,1)S(1)}, bf16[256,1024]{1,0:T(8,128)(2,1)S(1)}, u32[]{:S(2)}, u32[]{:S(2)}) collective-permute-start(bf16[256,1024]{1,0:T(8,128)(2,1)S(1)} %slice.252), channel_id=1, source_target_pairs={{2,0},{3,1},{130,128},{131,129},{258,256},{259,257},{386,384},{387... | collective-permute-start | bytes 1572872 | tf_op jit(solution)/shard_map/ppermute | solution.py:46
  102.3 1.9 %collective-permute-start.229 = (bf16[256,1024]{1,0:T(8,128)(2,1)S(1)}, bf16[256,1024]{1,0:T(8,128)(2,1)S(1)}, u32[]{:S(2)}, u32[]{:S(2)}) collective-permute-start(bf16[256,1024]{1,0:T(8,128)(2,1)S(1)} %slice.251), channel_id=1, source_target_pairs={{6,0},{7,1},{134,128},{135,129},{262,256},{263,257},{390,384},{391... | collective-permute-start | bytes 1572872 | tf_op jit(solution)/shard_map/ppermute | solution.py:46
  104.2 1.0 broadcast_select_fusion.2
  105.3 3.6 %collective-permute-start.224 = (bf16[512,256]{1,0:T(8,128)(2,1)S(1)}, bf16[512,256]{1,0:T(8,128)(2,1)S(1)}, u32[]{:S(2)}, u32[]{:S(2)}) collective-permute-start(bf16[512,256]{1,0:T(8,128)(2,1)S(1)} %broadcast_select_fusion.2), channel_id=1, source_target_pairs={{1,0},{0,1},{129,128},{128,129},{257,256},{256,257},{385,384},{384... | collective-permute-start | bytes 786440 | tf_op jit(solution)/shard_map/ppermute | solution.py:46
  108.9 1.1 collective-permute-done.224
  110.1 3.0 %left_operators.1 = bf16[2,16,64,512]{3,2,1,0:T(8,128)(2,1)S(1)} custom-call(s32[1,2]{1,0:T(1,128)S(1)} %copy-done, f32[2,3]{1,0:T(2,128)S(1)} %copy-done.5, s32[1,2,3]{2,1,0:T(2,128)S(1)} %copy-done.6, bf16[8,64,256]{2,1,0:T(8,128)(2,1)S(1)} %bitcast.18, bf16[8,64,256]{2,1,0:T(8,128)(2,1)S(1)} %bitcast.19, bf16[512,256]{1,0:T(8,128)(2,1)S(1)} %copy-done.1, ...), custom_call_target="tpu_custom_call" | custom-call | flops 2000000000 | bytes 4194304 | tf_op jit(solution)/shard_map/left_operators/pallas_call | solution.py:271
  113.1 4.4 %collective-permute-done.229.far_left = bf16[256,1024]{1,0:T(8,128)(2,1)S(1)} collective-permute-done((bf16[256,1024]{1,0:T(8,128)(2,1)S(1)}, bf16[256,1024]{1,0:T(8,128)(2,1)S(1)}, u32[]{:S(2)}, u32[]{:S(2)}) %collective-permute-start.229) | collective-permute-done | bytes 524320 | tf_op jit(solution)/shard_map/ppermute | solution.py:46
  117.5 1.8 %products.3 = bf16[2,256,1024]{2,1,0:T(8,128)(2,1)S(1)} custom-call(s32[1,2]{1,0:T(1,128)S(1)} %copy-done, bf16[2,1024,512]{2,1,0:T(8,128)(2,1)S(1)} %bitcast.16, bf16[512,1024]{1,0:T(8,128)(2,1)S(1)} %constant_dynamic-update-slice_fusion.held, bf16[512,1024]{1,0:T(8,128)(2,1)S(1)} %collective-permute-done.227.from_left, ...), custom_call_target="tpu_custom_call" | custom-call | flops 1073741824 | bytes 7340032 | tf_op jit(solution)/shard_map/products/pallas_call | solution.py:305
  119.3 4.1 %collective-permute-start.231 = (bf16[2,256,1024]{2,1,0:T(8,128)(2,1)S(1)}, bf16[2,256,1024]{2,1,0:T(8,128)(2,1)S(1)}, u32[]{:S(2)}, u32[]{:S(2)}) collective-permute-start(bf16[2,256,1024]{2,1,0:T(8,128)(2,1)S(1)} %products.3), channel_id=1, source_target_pairs={{1,0},{0,1},{129,128},{128,129},{257,256},{256,257},{385,384},{384... | collective-permute-start | bytes 3145736 | tf_op jit(solution)/shard_map/ppermute | solution.py:46
  123.5 1.8 %products.2 = bf16[2,256,1024]{2,1,0:T(8,128)(2,1)S(1)} custom-call(s32[1,2]{1,0:T(1,128)S(1)} %copy-done, bf16[2,1024,512]{2,1,0:T(8,128)(2,1)S(1)} %bitcast.17, bf16[512,1024]{1,0:T(8,128)(2,1)S(1)} %constant_dynamic-update-slice_fusion.held, bf16[512,1024]{1,0:T(8,128)(2,1)S(1)} %collective-permute-done.227.from_left, ...), custom_call_target="tpu_custom_call" | custom-call | flops 1073741824 | bytes 7340032 | tf_op jit(solution)/shard_map/products/pallas_call | solution.py:305
  125.3 0.4 collective-permute-done.231
  125.7 0.1 broadcast_select_fusion.1
  125.9 1.5 %pad_maximum_fusion.32 = bf16[2,256,2048]{2,1,0:T(8,128)(2,1)} fusion(bf16[2,256,1024]{2,1,0:T(8,128)(2,1)S(1)} %get-tuple-element.599, bf16[2,256,1024]{2,1,0:T(8,128)(2,1)S(1)} %get-tuple-element.598), kind=kLoop, calls=%fused_computation.128 | loop fusion | flops 4194304 | bytes 4194304 | tf_op jit(solution)/shard_map/concatenate | solution.py:413
  (33 shorter events, 0.3 us)
Async XLA Ops:
  1.1 12.2 %copy-start.8 = (bf16[64,1024]{1,0:T(8,128)(2,1)}, bf16[64,1024]{1,0:T(8,128)(2,1)S(1)}, u32[]{:S(2)}) copy-start(bf16[64,1024]{1,0:T(8,128)(2,1)S(1)} %get-tuple-element.600) | copy-start | bytes 393220
  1.1 11.5 %collective-permute-start.222 = (bf16[64,1024]{1,0:T(8,128)(2,1)S(1)}, bf16[64,1024]{1,0:T(8,128)(2,1)S(1)}, u32[]{:S(2)}, u32[]{:S(2)}) collective-permute-start(bf16[64,1024]{1,0:T(8,128)(2,1)S(1)} %get-tuple-element.601), channel_id=1, source_target_pairs={{1,0},{0,1},{129,128},{128,129},{257,256},{256,257},{385,384},{384... | collective-permute-start | bytes 393224 | tf_op jit(solution)/shard_map/ppermute | solution.py:46
  12.6 0.7 copy-start.11
  13.3 8.3 %collective-permute-start.175 = (bf16[256,256]{1,0:T(8,128)(2,1)S(1)}, bf16[256,256]{1,0:T(8,128)(2,1)}, u32[]{:S(2)}, u32[]{:S(2)}) collective-permute-start(bf16[256,256]{1,0:T(8,128)(2,1)S(1)} %pad_maximum_fusion.16), channel_id=1, source_target_pairs={{6,0},{7,1},{134,128},{135,129},{262,256},{263,257},{390,384},{391... | collective-permute-start | bytes 393224 | tf_op jit(solution)/shard_map/cond/branch_16_fun/ppermute | solution.py:46
  15.2 7.2 %collective-permute-start.176 = (bf16[128,256]{1,0:T(8,128)(2,1)S(1)}, bf16[128,256]{1,0:T(8,128)(2,1)}, u32[]{:S(2)}, u32[]{:S(2)}) collective-permute-start(bf16[128,256]{1,0:T(8,128)(2,1)S(1)} %get-tuple-element.550), channel_id=1, source_target_pairs={{2,0},{3,1},{130,128},{131,129},{258,256},{259,257},{386,384},{387... | collective-permute-start | bytes 196616 | tf_op jit(solution)/shard_map/cond/branch_16_fun/ppermute | solution.py:46
  22.5 50.1 %copy-start.9 = (bf16[128,256]{1,0:T(8,128)(2,1)}, bf16[128,256]{1,0:T(8,128)(2,1)S(1)}, u32[]{:S(2)}) copy-start(bf16[128,256]{1,0:T(8,128)(2,1)S(1)} %get-tuple-element.494) | copy-start | bytes 196612
  22.7 22.9 %collective-permute-start.107 = (bf16[128,1024]{1,0:T(8,128)(2,1)S(1)}, bf16[128,1024]{1,0:T(8,128)(2,1)}, u32[]{:S(2)}, u32[]{:S(2)}) collective-permute-start(bf16[128,1024]{1,0:T(8,128)(2,1)S(1)} %get-tuple-element.471), channel_id=1, source_target_pairs={{176,0},{177,1},{304,128},{305,129},{432,256},{433,257},{56,384},{... | collective-permute-start | bytes 786440 | tf_op jit(solution)/shard_map/cond/branch_27_fun/ppermute | solution.py:46
  27.7 18.7 %collective-permute-start.109 = (bf16[128,1024]{1,0:T(8,128)(2,1)}, bf16[128,1024]{1,0:T(8,128)(2,1)}, u32[]{:S(2)}, u32[]{:S(2)}) collective-permute-start(bf16[128,1024]{1,0:T(8,128)(2,1)} %get-tuple-element.472), channel_id=1, source_target_pairs={{256,0},{257,1},{384,128},{385,129},{8,256},{9,257},{136,384},{137... | collective-permute-start | bytes 786440 | tf_op jit(solution)/shard_map/cond/branch_27_fun/ppermute | solution.py:46
  30.0 16.4 %collective-permute-start.108 = (bf16[128,1024]{1,0:T(8,128)(2,1)}, bf16[128,1024]{1,0:T(8,128)(2,1)}, u32[]{:S(2)}, u32[]{:S(2)}) collective-permute-start(bf16[128,1024]{1,0:T(8,128)(2,1)} %get-tuple-element.472), channel_id=1, source_target_pairs={{264,0},{265,1},{392,128},{393,129},{0,256},{1,257},{128,384},{129... | collective-permute-start | bytes 786440 | tf_op jit(solution)/shard_map/cond/branch_27_fun/ppermute | solution.py:46
  37.5 6.6 %collective-permute-start.110 = (bf16[128,256]{1,0:T(8,128)(2,1)S(1)}, bf16[128,256]{1,0:T(8,128)(2,1)}, u32[]{:S(2)}, u32[]{:S(2)}) collective-permute-start(bf16[128,256]{1,0:T(8,128)(2,1)S(1)} %slice.200), channel_id=1, source_target_pairs={{6,0},{7,1},{134,128},{135,129},{262,256},{263,257},{390,384},{391... | collective-permute-start | bytes 196616 | tf_op jit(solution)/shard_map/cond/branch_27_fun/ppermute | solution.py:46
  46.3 14.8 %collective-permute-start.225 = (bf16[128,1024]{1,0:T(8,128)(2,1)}, bf16[128,1024]{1,0:T(8,128)(2,1)S(1)}, u32[]{:S(2)}, u32[]{:S(2)}) collective-permute-start(bf16[128,1024]{1,0:T(8,128)(2,1)} %get-tuple-element.500), channel_id=1, source_target_pairs={{264,0},{265,1},{392,128},{393,129},{0,256},{1,257},{128,384},{129... | collective-permute-start | bytes 786440 | tf_op jit(solution)/shard_map/ppermute | solution.py:46
  54.0 18.6 %collective-permute-start.226 = (bf16[128,1024]{1,0:T(8,128)(2,1)}, bf16[128,1024]{1,0:T(8,128)(2,1)S(1)}, u32[]{:S(2)}, u32[]{:S(2)}) collective-permute-start(bf16[128,1024]{1,0:T(8,128)(2,1)} %get-tuple-element.500), channel_id=1, source_target_pairs={{256,0},{257,1},{384,128},{385,129},{8,256},{9,257},{136,384},{137... | collective-permute-start | bytes 786440 | tf_op jit(solution)/shard_map/ppermute | solution.py:46
  62.1 47.9 %copy-start = (s32[1,2]{1,0:T(1,128)S(1)}, s32[1,2]{1,0:T(1,128)}, u32[]{:S(2)}) copy-start(s32[1,2]{1,0:T(1,128)} %partner_ref.5) | copy-start | bytes 28
  62.1 47.9 %copy-start.1 = (bf16[512,256]{1,0:T(8,128)(2,1)S(1)}, bf16[512,256]{1,0:T(8,128)(2,1)}, u32[]{:S(2)}) copy-start(bf16[512,256]{1,0:T(8,128)(2,1)} %proj_ref.1) | copy-start | bytes 786436
  62.1 47.9 %copy-start.2 = (f32[32,8,8]{0,2,1:T(8,128)S(1)}, f32[32,8,8]{0,2,1:T(8,128)}, u32[]{:S(2)}) copy-start(f32[32,8,8]{0,2,1:T(8,128)} %param.77) | copy-start | bytes 24580
  62.1 47.9 %copy-start.3 = (s32[32,16]{0,1:T(8,128)S(1)}, s32[32,16]{0,1:T(8,128)}, u32[]{:S(2)}) copy-start(s32[32,16]{0,1:T(8,128)} %param.75) | copy-start | bytes 6148
  62.1 47.9 %copy-start.4 = (f32[32,3]{0,1:T(4,128)S(1)}, f32[32,3]{0,1:T(4,128)}, u32[]{:S(2)}) copy-start(f32[32,3]{0,1:T(4,128)} %param.78) | copy-start | bytes 1156
  62.2 47.9 %copy-start.5 = (f32[2,3]{1,0:T(2,128)S(1)}, f32[2,3]{1,0:T(2,128)}, u32[]{:S(2)}) copy-start(f32[2,3]{1,0:T(2,128)} %b_ref.1) | copy-start | bytes 76
  62.2 47.9 %copy-start.6 = (s32[1,2,3]{2,1,0:T(2,128)S(1)}, s32[1,2,3]{2,1,0:T(2,128)}, u32[]{:S(2)}) copy-start(s32[1,2,3]{2,1,0:T(2,128)} %shift_ref.1) | copy-start | bytes 76
  62.2 47.9 %copy-start.7 = (s32[32]{0:T(128)S(1)}, s32[32]{0:T(128)}, u32[]{:S(2)}) copy-start(s32[32]{0:T(128)} %param.76) | copy-start | bytes 388
  72.6 26.1 %collective-permute-start.228 = (bf16[512,1024]{1,0:T(8,128)(2,1)S(1)}, bf16[512,1024]{1,0:T(8,128)(2,1)S(1)}, u32[]{:S(2)}, u32[]{:S(2)}) collective-permute-start(bf16[512,1024]{1,0:T(8,128)(2,1)S(1)} %constant_dynamic-update-slice_fusion.held), channel_id=1, source_target_pairs={{2,0},{3,1},{130,128},{131,129},{258,256},{259,257},{386,384},{387... | collective-permute-start | bytes 3145736 | tf_op jit(solution)/shard_map/ppermute | solution.py:46
  74.5 27.7 %collective-permute-start.227 = (bf16[512,1024]{1,0:T(8,128)(2,1)S(1)}, bf16[512,1024]{1,0:T(8,128)(2,1)S(1)}, u32[]{:S(2)}, u32[]{:S(2)}) collective-permute-start(bf16[512,1024]{1,0:T(8,128)(2,1)S(1)} %constant_dynamic-update-slice_fusion.held), channel_id=1, source_target_pairs={{6,0},{7,1},{134,128},{135,129},{262,256},{263,257},{390,384},{391... | collective-permute-start | bytes 3145736 | tf_op jit(solution)/shard_map/ppermute | solution.py:46
  80.3 23.9 %collective-permute-start.223 = (bf16[512,256]{1,0:T(8,128)(2,1)}, bf16[512,256]{1,0:T(8,128)(2,1)}, u32[]{:S(2)}, u32[]{:S(2)}) collective-permute-start(bf16[512,256]{1,0:T(8,128)(2,1)} %pad_maximum_fusion.34), channel_id=1, source_target_pairs={{8,1},{136,129},{264,257},{392,385},{1,8},{129,136},{257,264},{385... | collective-permute-start | bytes 786440 | tf_op jit(solution)/shard_map/ppermute | solution.py:46
  86.1 18.2 %copy-start.10 = (bf16[128,256]{1,0:T(8,128)(2,1)S(1)}, bf16[128,256]{1,0:T(8,128)(2,1)}, u32[]{:S(2)}) copy-start(bf16[128,256]{1,0:T(8,128)(2,1)} %copy-done.9) | copy-start | bytes 196612
  98.8 14.3 %collective-permute-start.230 = (bf16[256,1024]{1,0:T(8,128)(2,1)S(1)}, bf16[256,1024]{1,0:T(8,128)(2,1)S(1)}, u32[]{:S(2)}, u32[]{:S(2)}) collective-permute-start(bf16[256,1024]{1,0:T(8,128)(2,1)S(1)} %slice.252), channel_id=1, source_target_pairs={{2,0},{3,1},{130,128},{131,129},{258,256},{259,257},{386,384},{387... | collective-permute-start | bytes 1572872 | tf_op jit(solution)/shard_map/ppermute | solution.py:46
  102.3 15.2 %collective-permute-start.229 = (bf16[256,1024]{1,0:T(8,128)(2,1)S(1)}, bf16[256,1024]{1,0:T(8,128)(2,1)S(1)}, u32[]{:S(2)}, u32[]{:S(2)}) collective-permute-start(bf16[256,1024]{1,0:T(8,128)(2,1)S(1)} %slice.251), channel_id=1, source_target_pairs={{6,0},{7,1},{134,128},{135,129},{262,256},{263,257},{390,384},{391... | collective-permute-start | bytes 1572872 | tf_op jit(solution)/shard_map/ppermute | solution.py:46
  105.3 4.8 %collective-permute-start.224 = (bf16[512,256]{1,0:T(8,128)(2,1)S(1)}, bf16[512,256]{1,0:T(8,128)(2,1)S(1)}, u32[]{:S(2)}, u32[]{:S(2)}) collective-permute-start(bf16[512,256]{1,0:T(8,128)(2,1)S(1)} %broadcast_select_fusion.2), channel_id=1, source_target_pairs={{1,0},{0,1},{129,128},{128,129},{257,256},{256,257},{385,384},{384... | collective-permute-start | bytes 786440 | tf_op jit(solution)/shard_map/ppermute | solution.py:46
  119.3 6.4 %collective-permute-start.231 = (bf16[2,256,1024]{2,1,0:T(8,128)(2,1)S(1)}, bf16[2,256,1024]{2,1,0:T(8,128)(2,1)S(1)}, u32[]{:S(2)}, u32[]{:S(2)}) collective-permute-start(bf16[2,256,1024]{2,1,0:T(8,128)(2,1)S(1)} %products.3), channel_id=1, source_target_pairs={{1,0},{0,1},{129,128},{128,129},{257,256},{256,257},{385,384},{384... | collective-permute-start | bytes 3145736 | tf_op jit(solution)/shard_map/ppermute | solution.py:46

commit v2 on v1

--- a/solution.py
+++ b/solution.py
@@ -70,7 +70,7 @@
         self.z = self.z_hi * Z_LO + (point >> 3)
         distances = [(partner[0, v] - point) & (POINTS - 1) for v in range(2)]
         along = [d & (Y - 1) for d in distances]
-        hops = [jnp.minimum(d, Y - d) for d in along]
+        hops = [jnp.where(d == Y // 2, 2, jnp.minimum(d, Y - d)) for d in along]
         swapped = hops[0] > hops[1]
         self.swap = jnp.where(swapped, 1, 0)
         self.distances = [
@@ -365,7 +365,7 @@
         return (
             toward_partner(lane, distance),
             held_first,
-            from_x(onward[half_rows:], -1),
+            from_x(onward, -1),
         )
 
     moved_first, one_back, one_on = lax.switch(
@@ -387,7 +387,9 @@
     from_left, from_right = from_x(held, -1), from_x(held, 1)
     far_left = from_x(from_left[: 2 * half_rows], -1)
     far_right = from_x(from_right[2 * half_rows :], 1)
-    own = jnp.concatenate([bands_of(lane, 0), one_back[:half_rows], two_back, one_on], axis=0)
+    own = jnp.concatenate(
+        [bands_of(lane, 0), one_back[:half_rows], two_back[half_rows:], one_on], axis=0
+    )
     own = jnp.where(core == z_hi, own, from_other_half(own))
     other = from_other_core(own)
     own_shape = (X * CORE, 2 * row_count, chip_bands)

time: 128 us -> 128 us (level)
  the two profiles are of different devices: /device:TPU:1 before, /device:TPU:33 now
where the time goes in v2:
time: 128 us; the launch traced here: 127 us
  starting transfers between devices  65.9 us (51%)
  waiting for transfers between devices  41.5 us (32%)
  Pallas kernels  6.62 us (5%)
  local copies, waits for them, and re-layouts  5.97 us (5%)
  other arithmetic  5.15 us (4%)
  between operations  1.54 us (1%)
    ppermute x17, starting transfers between devices, moved(): return lax.ppermute(block, AXES, route(source_of))  65.9 us
    ppermute x17, waiting for transfers between devices, moved(): return lax.ppermute(block, AXES, route(source_of))  41.5 us
    pallas_call x2, Pallas kernels, products(): pl.pallas_call(product_kernel, grid=(1,), out_shape=jax.ShapeDtypeStruct(...  3.65 us
    pallas_call x1, Pallas kernels, left_operators(): pl.pallas_call(left_kernel, out_shape=jax.ShapeDtypeStruct((2, SLABS, 2 *...  2.97 us
    unnamed x31, local copies, waits for them, and re-layouts  2.66 us
  transfers between devices with their start and end apart: 17, of which 10 were waited for; matrix products, arithmetic and copies ran while one was open for 6% of the time, Pallas kernels for 4%

profile of v2, /device:TPU:33, one launch (start us, length us, event | category | flops | bytes accessed | tf_op | source)
XLA Modules:
  0.0 126.9 jit_solution(13398956121421228257)
XLA Ops:
  0.0 1.0 copy.10
  1.1 0.0 copy-start.8
  1.1 2.6 %collective-permute-start.222 = (bf16[64,1024]{1,0:T(8,128)(2,1)S(1)}, bf16[64,1024]{1,0:T(8,128)(2,1)S(1)}, u32[]{:S(2)}, u32[]{:S(2)}) collective-permute-start(bf16[64,1024]{1,0:T(8,128)(2,1)S(1)} %get-tuple-element.602), channel_id=1, source_target_pairs={{1,0},{0,1},{129,128},{128,129},{257,256},{256,257},{385,384},{384... | collective-permute-start | bytes 393224 | tf_op jit(solution)/shard_map/ppermute | solution.py:46
  3.7 1.3 %fusion.1 = (s32[1,1]{1,0:T(1,128)}, s32[1,1]{1,0:T(1,128)}) fusion(s32[1,2]{1,0:T(1,128)} %partner_ref.5), kind=kLoop, calls=%fused_computation.143 | loop fusion | bytes 16 | tf_op jit(solution)/shard_map/slice | solution.py:71
  6.2 0.6 copy-done.13
  6.8 17.2 %conditional.2 = (bf16[128,1024]{1,0:T(8,128)(2,1)}, bf16[256,256]{1,0:T(8,128)(2,1)}, bf16[128,256]{1,0:T(8,128)(2,1)}, bf16[128,256]{1,0:T(8,128)(2,1)S(1)}) conditional(s32[]{:T(128)} %clamp.6, (bf16[128,1024]{1,0:T(8,128)(2,1)S(1)}, s32[]{:T(128)}) %tuple.325, (bf16[128,1024]{1,0:T(8,128)(2,1)S(1)}, ...), branch_computations={%region_0.1_spmd, %region_1.2_spmd, %region_2.3_spmd, %region_3.4_... | conditional | flops 262192 | bytes 2622105 | solution.py:371
  6.8 5.9 %collective-permute-start.219 = (bf16[128,1024]{1,0:T(8,128)(2,1)S(1)}, bf16[128,1024]{1,0:T(8,128)(2,1)}, u32[]{:S(2)}, u32[]{:S(2)}) collective-permute-start(bf16[128,1024]{1,0:T(8,128)(2,1)S(1)} %get-tuple-element.389), channel_id=1, source_target_pairs={{240,0},{241,1},{368,128},{369,129},{496,256},{497,257},{120,384},... | collective-permute-start | bytes 786440 | tf_op jit(solution)/shard_map/cond/branch_31_fun/ppermute | solution.py:46
  12.8 3.1 %collective-permute-start.220 = (bf16[256,256]{1,0:T(8,128)(2,1)S(1)}, bf16[256,256]{1,0:T(8,128)(2,1)}, u32[]{:S(2)}, u32[]{:S(2)}) collective-permute-start(bf16[256,256]{1,0:T(8,128)(2,1)S(1)} %pad_maximum_fusion.31), channel_id=1, source_target_pairs={{6,0},{7,1},{134,128},{135,129},{262,256},{263,257},{390,384},{391... | collective-permute-start | bytes 393224 | tf_op jit(solution)/shard_map/cond/branch_31_fun/ppermute | solution.py:46
  16.0 3.4 %collective-permute-start.221 = (bf16[128,256]{1,0:T(8,128)(2,1)S(1)}, bf16[128,256]{1,0:T(8,128)(2,1)}, u32[]{:S(2)}, u32[]{:S(2)}) collective-permute-start(bf16[128,256]{1,0:T(8,128)(2,1)S(1)} %get-tuple-element.596), channel_id=1, source_target_pairs={{2,0},{3,1},{130,128},{131,129},{258,256},{259,257},{386,384},{387... | collective-permute-start | bytes 196616 | tf_op jit(solution)/shard_map/cond/branch_31_fun/ppermute | solution.py:46
  19.4 0.5 collective-permute-done.220
  19.9 0.8 slice.249
  20.7 0.4 collective-permute-done.221
  21.1 2.9 %collective-permute-done.219 = bf16[128,1024]{1,0:T(8,128)(2,1)} collective-permute-done((bf16[128,1024]{1,0:T(8,128)(2,1)S(1)}, bf16[128,1024]{1,0:T(8,128)(2,1)}, u32[]{:S(2)}, u32[]{:S(2)}) %collective-permute-start.219) | collective-permute-done | bytes 262176 | tf_op jit(solution)/shard_map/cond/branch_31_fun/ppermute | solution.py:46
  24.0 25.8 %conditional.3 = (bf16[128,1024]{1,0:T(8,128)(2,1)}, bf16[128,1024]{1,0:T(8,128)(2,1)}, bf16[128,1024]{1,0:T(8,128)(2,1)}, bf16[128,256]{1,0:T(8,128)(2,1)S(1)}) conditional(s32[]{:T(128)} %clamp.7, (bf16[128,1024]{1,0:T(8,128)(2,1)S(1)}, bf16[128,1024]{1,0:T(8,128)(2,1)}, bf16[256,256]{1,0:T(8,128)(2,1)}) %tuple.327, ...), branch_computations={%region_32.33_spmd, %region_33.34_spmd, %region_34.35_spmd, %regio... | conditional | bytes 3801280 | solution.py:376
  24.0 5.2 %collective-permute-start.91 = (bf16[128,1024]{1,0:T(8,128)(2,1)S(1)}, bf16[128,1024]{1,0:T(8,128)(2,1)}, u32[]{:S(2)}, u32[]{:S(2)}) collective-permute-start(bf16[128,1024]{1,0:T(8,128)(2,1)S(1)} %get-tuple-element.460), channel_id=1, source_target_pairs={{112,0},{113,1},{240,128},{241,129},{368,256},{369,257},{496,384},... | collective-permute-start | bytes 786440 | tf_op jit(solution)/shard_map/cond/branch_23_fun/ppermute | solution.py:46
  29.2 3.4 %collective-permute-start.93 = (bf16[128,1024]{1,0:T(8,128)(2,1)}, bf16[128,1024]{1,0:T(8,128)(2,1)}, u32[]{:S(2)}, u32[]{:S(2)}) collective-permute-start(bf16[128,1024]{1,0:T(8,128)(2,1)} %get-tuple-element.461), channel_id=1, source_target_pairs={{256,0},{257,1},{384,128},{385,129},{8,256},{9,257},{136,384},{137... | collective-permute-start | bytes 786440 | tf_op jit(solution)/shard_map/cond/branch_23_fun/ppermute | solution.py:46
  32.6 2.8 %collective-permute-start.92 = (bf16[128,1024]{1,0:T(8,128)(2,1)}, bf16[128,1024]{1,0:T(8,128)(2,1)}, u32[]{:S(2)}, u32[]{:S(2)}) collective-permute-start(bf16[128,1024]{1,0:T(8,128)(2,1)} %get-tuple-element.461), channel_id=1, source_target_pairs={{264,0},{265,1},{392,128},{393,129},{0,256},{1,257},{128,384},{129... | collective-permute-start | bytes 786440 | tf_op jit(solution)/shard_map/cond/branch_23_fun/ppermute | solution.py:46
  35.4 3.1 %collective-permute-start.94 = (bf16[256,256]{1,0:T(8,128)(2,1)}, bf16[256,256]{1,0:T(8,128)(2,1)S(1)}, u32[]{:S(2)}, u32[]{:S(2)}) collective-permute-start(bf16[256,256]{1,0:T(8,128)(2,1)} %get-tuple-element.462), channel_id=1, source_target_pairs={{6,0},{7,1},{134,128},{135,129},{262,256},{263,257},{390,384},{391... | collective-permute-start | bytes 393224 | tf_op jit(solution)/shard_map/cond/branch_23_fun/ppermute | solution.py:46
  38.6 4.4 %collective-permute-done.94 = bf16[256,256]{1,0:T(8,128)(2,1)S(1)} collective-permute-done((bf16[256,256]{1,0:T(8,128)(2,1)}, bf16[256,256]{1,0:T(8,128)(2,1)S(1)}, u32[]{:S(2)}, u32[]{:S(2)}) %collective-permute-start.94) | collective-permute-done | bytes 131104 | tf_op jit(solution)/shard_map/cond/branch_23_fun/ppermute | solution.py:46
  43.0 6.8 %collective-permute-done.93 = bf16[128,1024]{1,0:T(8,128)(2,1)} collective-permute-done((bf16[128,1024]{1,0:T(8,128)(2,1)}, bf16[128,1024]{1,0:T(8,128)(2,1)}, u32[]{:S(2)}, u32[]{:S(2)}) %collective-permute-start.93) | collective-permute-done | bytes 262176 | tf_op jit(solution)/shard_map/cond/branch_23_fun/ppermute | solution.py:46
  49.8 4.0 %collective-permute-start.225 = (bf16[128,1024]{1,0:T(8,128)(2,1)}, bf16[128,1024]{1,0:T(8,128)(2,1)S(1)}, u32[]{:S(2)}, u32[]{:S(2)}) collective-permute-start(bf16[128,1024]{1,0:T(8,128)(2,1)} %get-tuple-element.501), channel_id=1, source_target_pairs={{264,0},{265,1},{392,128},{393,129},{0,256},{1,257},{128,384},{129... | collective-permute-start | bytes 786440 | tf_op jit(solution)/shard_map/ppermute | solution.py:46
  53.8 4.3 %collective-permute-start.226 = (bf16[128,1024]{1,0:T(8,128)(2,1)}, bf16[128,1024]{1,0:T(8,128)(2,1)S(1)}, u32[]{:S(2)}, u32[]{:S(2)}) collective-permute-start(bf16[128,1024]{1,0:T(8,128)(2,1)} %get-tuple-element.501), channel_id=1, source_target_pairs={{256,0},{257,1},{384,128},{385,129},{8,256},{9,257},{136,384},{137... | collective-permute-start | bytes 786440 | tf_op jit(solution)/shard_map/ppermute | solution.py:46
  58.1 1.0 constant_dynamic-update-slice_fusion.3
  59.1 9.7 %collective-permute-done.225 = bf16[128,1024]{1,0:T(8,128)(2,1)S(1)} collective-permute-done((bf16[128,1024]{1,0:T(8,128)(2,1)}, bf16[128,1024]{1,0:T(8,128)(2,1)S(1)}, u32[]{:S(2)}, u32[]{:S(2)}) %collective-permute-start.225) | collective-permute-done | bytes 262176 | tf_op jit(solution)/shard_map/ppermute | solution.py:46
  68.8 1.0 constant_dynamic-update-slice_fusion.1
  69.8 0.0 copy-start.1
  69.8 0.0 copy-start.2
  69.8 0.0 copy-start.5
  69.8 0.0 copy-start.6
  69.9 4.5 %collective-permute-start.228 = (bf16[512,1024]{1,0:T(8,128)(2,1)S(1)}, bf16[512,1024]{1,0:T(8,128)(2,1)S(1)}, u32[]{:S(2)}, u32[]{:S(2)}) collective-permute-start(bf16[512,1024]{1,0:T(8,128)(2,1)S(1)} %constant_dynamic-update-slice_fusion.held), channel_id=1, source_target_pairs={{2,0},{3,1},{130,128},{131,129},{258,256},{259,257},{386,384},{387... | collective-permute-start | bytes 3145736 | tf_op jit(solution)/shard_map/ppermute | solution.py:46
  74.4 1.9 %collective-permute-start.227 = (bf16[512,1024]{1,0:T(8,128)(2,1)S(1)}, bf16[512,1024]{1,0:T(8,128)(2,1)S(1)}, u32[]{:S(2)}, u32[]{:S(2)}) collective-permute-start(bf16[512,1024]{1,0:T(8,128)(2,1)S(1)} %constant_dynamic-update-slice_fusion.held), channel_id=1, source_target_pairs={{6,0},{7,1},{134,128},{135,129},{262,256},{263,257},{390,384},{391... | collective-permute-start | bytes 3145736 | tf_op jit(solution)/shard_map/ppermute | solution.py:46
  76.3 0.8 fusion
  77.1 1.6 %pad_maximum_fusion.34 = bf16[512,256]{1,0:T(8,128)(2,1)} fusion(bf16[128,256]{1,0:T(8,128)(2,1)} %get-tuple-element.499, bf16[128,256]{1,0:T(8,128)(2,1)} %copy-done.9, bf16[128,256]{1,0:T(8,128)(2,1)} %copy-done.11, bf16[128,256]{1,0:T(8,128)(2,1)S(1)} %fusion), kind=kLoop, calls=%fused_computation.134 | loop fusion | flops 1048576 | bytes 524288 | tf_op jit(solution)/shard_map/concatenate | solution.py:390
  78.7 6.6 %collective-permute-start.223 = (bf16[512,256]{1,0:T(8,128)(2,1)}, bf16[512,256]{1,0:T(8,128)(2,1)}, u32[]{:S(2)}, u32[]{:S(2)}) collective-permute-start(bf16[512,256]{1,0:T(8,128)(2,1)} %pad_maximum_fusion.34), channel_id=1, source_target_pairs={{8,1},{136,129},{264,257},{392,385},{1,8},{129,136},{257,264},{385... | collective-permute-start | bytes 786440 | tf_op jit(solution)/shard_map/ppermute | solution.py:46
  85.3 11.0 %collective-permute-done.228.from_right = bf16[512,1024]{1,0:T(8,128)(2,1)S(1)} collective-permute-done((bf16[512,1024]{1,0:T(8,128)(2,1)S(1)}, bf16[512,1024]{1,0:T(8,128)(2,1)S(1)}, u32[]{:S(2)}, u32[]{:S(2)}) %collective-permute-start.228) | collective-permute-done | bytes 1048608 | tf_op jit(solution)/shard_map/ppermute | solution.py:46
  96.4 5.3 %collective-permute-start.230 = (bf16[256,1024]{1,0:T(8,128)(2,1)S(1)}, bf16[256,1024]{1,0:T(8,128)(2,1)S(1)}, u32[]{:S(2)}, u32[]{:S(2)}) collective-permute-start(bf16[256,1024]{1,0:T(8,128)(2,1)S(1)} %slice.285), channel_id=1, source_target_pairs={{2,0},{3,1},{130,128},{131,129},{258,256},{259,257},{386,384},{387... | collective-permute-start | bytes 1572872 | tf_op jit(solution)/shard_map/ppermute | solution.py:46
  101.8 1.9 %collective-permute-start.229 = (bf16[256,1024]{1,0:T(8,128)(2,1)S(1)}, bf16[256,1024]{1,0:T(8,128)(2,1)S(1)}, u32[]{:S(2)}, u32[]{:S(2)}) collective-permute-start(bf16[256,1024]{1,0:T(8,128)(2,1)S(1)} %slice.284), channel_id=1, source_target_pairs={{6,0},{7,1},{134,128},{135,129},{262,256},{263,257},{390,384},{391... | collective-permute-start | bytes 1572872 | tf_op jit(solution)/shard_map/ppermute | solution.py:46
  103.7 1.0 broadcast_select_fusion.2
  104.8 3.5 %collective-permute-start.224 = (bf16[512,256]{1,0:T(8,128)(2,1)S(1)}, bf16[512,256]{1,0:T(8,128)(2,1)S(1)}, u32[]{:S(2)}, u32[]{:S(2)}) collective-permute-start(bf16[512,256]{1,0:T(8,128)(2,1)S(1)} %broadcast_select_fusion.2), channel_id=1, source_target_pairs={{1,0},{0,1},{129,128},{128,129},{257,256},{256,257},{385,384},{384... | collective-permute-start | bytes 786440 | tf_op jit(solution)/shard_map/ppermute | solution.py:46
  108.2 1.1 collective-permute-done.224
  109.4 3.0 %left_operators.1 = bf16[2,16,64,512]{3,2,1,0:T(8,128)(2,1)S(1)} custom-call(s32[1,2]{1,0:T(1,128)S(1)} %copy-done, f32[2,3]{1,0:T(2,128)S(1)} %copy-done.5, s32[1,2,3]{2,1,0:T(2,128)S(1)} %copy-done.6, bf16[8,64,256]{2,1,0:T(8,128)(2,1)S(1)} %bitcast.18, bf16[8,64,256]{2,1,0:T(8,128)(2,1)S(1)} %bitcast.19, bf16[512,256]{1,0:T(8,128)(2,1)S(1)} %copy-done.1, ...), custom_call_target="tpu_custom_call" | custom-call | flops 2000000000 | bytes 4194304 | tf_op jit(solution)/shard_map/left_operators/pallas_call | solution.py:271
  112.4 4.2 %collective-permute-done.229.far_left = bf16[256,1024]{1,0:T(8,128)(2,1)S(1)} collective-permute-done((bf16[256,1024]{1,0:T(8,128)(2,1)S(1)}, bf16[256,1024]{1,0:T(8,128)(2,1)S(1)}, u32[]{:S(2)}, u32[]{:S(2)}) %collective-permute-start.229) | collective-permute-done | bytes 524320 | tf_op jit(solution)/shard_map/ppermute | solution.py:46
  116.6 1.8 %products.3 = bf16[2,256,1024]{2,1,0:T(8,128)(2,1)S(1)} custom-call(s32[1,2]{1,0:T(1,128)S(1)} %copy-done, bf16[2,1024,512]{2,1,0:T(8,128)(2,1)S(1)} %bitcast.16, bf16[512,1024]{1,0:T(8,128)(2,1)S(1)} %constant_dynamic-update-slice_fusion.held, bf16[512,1024]{1,0:T(8,128)(2,1)S(1)} %collective-permute-done.227.from_left, ...), custom_call_target="tpu_custom_call" | custom-call | flops 1073741824 | bytes 7340032 | tf_op jit(solution)/shard_map/products/pallas_call | solution.py:305
  118.5 4.5 %collective-permute-start.231 = (bf16[2,256,1024]{2,1,0:T(8,128)(2,1)S(1)}, bf16[2,256,1024]{2,1,0:T(8,128)(2,1)S(1)}, u32[]{:S(2)}, u32[]{:S(2)}) collective-permute-start(bf16[2,256,1024]{2,1,0:T(8,128)(2,1)S(1)} %products.3), channel_id=1, source_target_pairs={{1,0},{0,1},{129,128},{128,129},{257,256},{256,257},{385,384},{384... | collective-permute-start | bytes 3145736 | tf_op jit(solution)/shard_map/ppermute | solution.py:46
  123.0 1.8 %products.2 = bf16[2,256,1024]{2,1,0:T(8,128)(2,1)S(1)} custom-call(s32[1,2]{1,0:T(1,128)S(1)} %copy-done, bf16[2,1024,512]{2,1,0:T(8,128)(2,1)S(1)} %bitcast.17, bf16[512,1024]{1,0:T(8,128)(2,1)S(1)} %constant_dynamic-update-slice_fusion.held, bf16[512,1024]{1,0:T(8,128)(2,1)S(1)} %collective-permute-done.227.from_left, ...), custom_call_target="tpu_custom_call" | custom-call | flops 1073741824 | bytes 7340032 | tf_op jit(solution)/shard_map/products/pallas_call | solution.py:305
  124.8 0.4 collective-permute-done.231
  125.2 0.1 broadcast_select_fusion.1
  125.4 1.5 %pad_maximum_fusion.32 = bf16[2,256,2048]{2,1,0:T(8,128)(2,1)} fusion(bf16[2,256,1024]{2,1,0:T(8,128)(2,1)S(1)} %get-tuple-element.600, bf16[2,256,1024]{2,1,0:T(8,128)(2,1)S(1)} %get-tuple-element.599), kind=kLoop, calls=%fused_computation.128 | loop fusion | flops 4194304 | bytes 4194304 | tf_op jit(solution)/shard_map/concatenate | solution.py:415
  (38 shorter events, 0.3 us)
Async XLA Ops:
  1.1 5.7 %copy-start.8 = (bf16[64,1024]{1,0:T(8,128)(2,1)}, bf16[64,1024]{1,0:T(8,128)(2,1)S(1)}, u32[]{:S(2)}) copy-start(bf16[64,1024]{1,0:T(8,128)(2,1)S(1)} %get-tuple-element.601) | copy-start | bytes 393220
  1.1 5.0 %collective-permute-start.222 = (bf16[64,1024]{1,0:T(8,128)(2,1)S(1)}, bf16[64,1024]{1,0:T(8,128)(2,1)S(1)}, u32[]{:S(2)}, u32[]{:S(2)}) collective-permute-start(bf16[64,1024]{1,0:T(8,128)(2,1)S(1)} %get-tuple-element.602), channel_id=1, source_target_pairs={{1,0},{0,1},{129,128},{128,129},{257,256},{256,257},{385,384},{384... | collective-permute-start | bytes 393224 | tf_op jit(solution)/shard_map/ppermute | solution.py:46
  6.1 0.7 copy-start.13
  6.8 17.2 %collective-permute-start.219 = (bf16[128,1024]{1,0:T(8,128)(2,1)S(1)}, bf16[128,1024]{1,0:T(8,128)(2,1)}, u32[]{:S(2)}, u32[]{:S(2)}) collective-permute-start(bf16[128,1024]{1,0:T(8,128)(2,1)S(1)} %get-tuple-element.389), channel_id=1, source_target_pairs={{240,0},{241,1},{368,128},{369,129},{496,256},{497,257},{120,384},... | collective-permute-start | bytes 786440 | tf_op jit(solution)/shard_map/cond/branch_31_fun/ppermute | solution.py:46
  12.8 7.0 %collective-permute-start.220 = (bf16[256,256]{1,0:T(8,128)(2,1)S(1)}, bf16[256,256]{1,0:T(8,128)(2,1)}, u32[]{:S(2)}, u32[]{:S(2)}) collective-permute-start(bf16[256,256]{1,0:T(8,128)(2,1)S(1)} %pad_maximum_fusion.31), channel_id=1, source_target_pairs={{6,0},{7,1},{134,128},{135,129},{262,256},{263,257},{390,384},{391... | collective-permute-start | bytes 393224 | tf_op jit(solution)/shard_map/cond/branch_31_fun/ppermute | solution.py:46
  16.0 5.1 %collective-permute-start.221 = (bf16[128,256]{1,0:T(8,128)(2,1)S(1)}, bf16[128,256]{1,0:T(8,128)(2,1)}, u32[]{:S(2)}, u32[]{:S(2)}) collective-permute-start(bf16[128,256]{1,0:T(8,128)(2,1)S(1)} %get-tuple-element.596), channel_id=1, source_target_pairs={{2,0},{3,1},{130,128},{131,129},{258,256},{259,257},{386,384},{387... | collective-permute-start | bytes 196616 | tf_op jit(solution)/shard_map/cond/branch_31_fun/ppermute | solution.py:46
  24.0 45.8 %copy-start.11 = (bf16[128,256]{1,0:T(8,128)(2,1)}, bf16[128,256]{1,0:T(8,128)(2,1)S(1)}, u32[]{:S(2)}) copy-start(bf16[128,256]{1,0:T(8,128)(2,1)S(1)} %get-tuple-element.495) | copy-start | bytes 196612
  24.0 19.0 %collective-permute-start.91 = (bf16[128,1024]{1,0:T(8,128)(2,1)S(1)}, bf16[128,1024]{1,0:T(8,128)(2,1)}, u32[]{:S(2)}, u32[]{:S(2)}) collective-permute-start(bf16[128,1024]{1,0:T(8,128)(2,1)S(1)} %get-tuple-element.460), channel_id=1, source_target_pairs={{112,0},{113,1},{240,128},{241,129},{368,256},{369,257},{496,384},... | collective-permute-start | bytes 786440 | tf_op jit(solution)/shard_map/cond/branch_23_fun/ppermute | solution.py:46
  29.2 20.6 %collective-permute-start.93 = (bf16[128,1024]{1,0:T(8,128)(2,1)}, bf16[128,1024]{1,0:T(8,128)(2,1)}, u32[]{:S(2)}, u32[]{:S(2)}) collective-permute-start(bf16[128,1024]{1,0:T(8,128)(2,1)} %get-tuple-element.461), channel_id=1, source_target_pairs={{256,0},{257,1},{384,128},{385,129},{8,256},{9,257},{136,384},{137... | collective-permute-start | bytes 786440 | tf_op jit(solution)/shard_map/cond/branch_23_fun/ppermute | solution.py:46
  32.6 17.2 %collective-permute-start.92 = (bf16[128,1024]{1,0:T(8,128)(2,1)}, bf16[128,1024]{1,0:T(8,128)(2,1)}, u32[]{:S(2)}, u32[]{:S(2)}) collective-permute-start(bf16[128,1024]{1,0:T(8,128)(2,1)} %get-tuple-element.461), channel_id=1, source_target_pairs={{264,0},{265,1},{392,128},{393,129},{0,256},{1,257},{128,384},{129... | collective-permute-start | bytes 786440 | tf_op jit(solution)/shard_map/cond/branch_23_fun/ppermute | solution.py:46
  35.4 7.5 %collective-permute-start.94 = (bf16[256,256]{1,0:T(8,128)(2,1)}, bf16[256,256]{1,0:T(8,128)(2,1)S(1)}, u32[]{:S(2)}, u32[]{:S(2)}) collective-permute-start(bf16[256,256]{1,0:T(8,128)(2,1)} %get-tuple-element.462), channel_id=1, source_target_pairs={{6,0},{7,1},{134,128},{135,129},{262,256},{263,257},{390,384},{391... | collective-permute-start | bytes 393224 | tf_op jit(solution)/shard_map/cond/branch_23_fun/ppermute | solution.py:46
  49.8 20.1 %copy-start.9 = (bf16[128,256]{1,0:T(8,128)(2,1)}, bf16[128,256]{1,0:T(8,128)(2,1)S(1)}, u32[]{:S(2)}) copy-start(bf16[128,256]{1,0:T(8,128)(2,1)S(1)} %get-tuple-element.498) | copy-start | bytes 196612
  49.8 18.9 %collective-permute-start.225 = (bf16[128,1024]{1,0:T(8,128)(2,1)}, bf16[128,1024]{1,0:T(8,128)(2,1)S(1)}, u32[]{:S(2)}, u32[]{:S(2)}) collective-permute-start(bf16[128,1024]{1,0:T(8,128)(2,1)} %get-tuple-element.501), channel_id=1, source_target_pairs={{264,0},{265,1},{392,128},{393,129},{0,256},{1,257},{128,384},{129... | collective-permute-start | bytes 786440 | tf_op jit(solution)/shard_map/ppermute | solution.py:46
  53.8 16.0 %collective-permute-start.226 = (bf16[128,1024]{1,0:T(8,128)(2,1)}, bf16[128,1024]{1,0:T(8,128)(2,1)S(1)}, u32[]{:S(2)}, u32[]{:S(2)}) collective-permute-start(bf16[128,1024]{1,0:T(8,128)(2,1)} %get-tuple-element.501), channel_id=1, source_target_pairs={{256,0},{257,1},{384,128},{385,129},{8,256},{9,257},{136,384},{137... | collective-permute-start | bytes 786440 | tf_op jit(solution)/shard_map/ppermute | solution.py:46
  69.7 39.7 %copy-start = (s32[1,2]{1,0:T(1,128)S(1)}, s32[1,2]{1,0:T(1,128)}, u32[]{:S(2)}) copy-start(s32[1,2]{1,0:T(1,128)} %partner_ref.5) | copy-start | bytes 28
  69.8 39.6 %copy-start.1 = (bf16[512,256]{1,0:T(8,128)(2,1)S(1)}, bf16[512,256]{1,0:T(8,128)(2,1)}, u32[]{:S(2)}) copy-start(bf16[512,256]{1,0:T(8,128)(2,1)} %proj_ref.1) | copy-start | bytes 786436
  69.8 39.6 %copy-start.2 = (f32[32,8,8]{0,2,1:T(8,128)S(1)}, f32[32,8,8]{0,2,1:T(8,128)}, u32[]{:S(2)}) copy-start(f32[32,8,8]{0,2,1:T(8,128)} %param.77) | copy-start | bytes 24580
  69.8 39.6 %copy-start.3 = (s32[32,16]{0,1:T(8,128)S(1)}, s32[32,16]{0,1:T(8,128)}, u32[]{:S(2)}) copy-start(s32[32,16]{0,1:T(8,128)} %param.75) | copy-start | bytes 6148
  69.8 39.6 %copy-start.4 = (f32[32,3]{0,1:T(4,128)S(1)}, f32[32,3]{0,1:T(4,128)}, u32[]{:S(2)}) copy-start(f32[32,3]{0,1:T(4,128)} %param.78) | copy-start | bytes 1156
  69.8 39.6 %copy-start.5 = (f32[2,3]{1,0:T(2,128)S(1)}, f32[2,3]{1,0:T(2,128)}, u32[]{:S(2)}) copy-start(f32[2,3]{1,0:T(2,128)} %b_ref.1) | copy-start | bytes 76
  69.8 39.6 %copy-start.6 = (s32[1,2,3]{2,1,0:T(2,128)S(1)}, s32[1,2,3]{2,1,0:T(2,128)}, u32[]{:S(2)}) copy-start(s32[1,2,3]{2,1,0:T(2,128)} %shift_ref.1) | copy-start | bytes 76
  69.8 39.6 %copy-start.7 = (s32[32]{0:T(128)S(1)}, s32[32]{0:T(128)}, u32[]{:S(2)}) copy-start(s32[32]{0:T(128)} %param.76) | copy-start | bytes 388
  69.9 26.5 %collective-permute-start.228 = (bf16[512,1024]{1,0:T(8,128)(2,1)S(1)}, bf16[512,1024]{1,0:T(8,128)(2,1)S(1)}, u32[]{:S(2)}, u32[]{:S(2)}) collective-permute-start(bf16[512,1024]{1,0:T(8,128)(2,1)S(1)} %constant_dynamic-update-slice_fusion.held), channel_id=1, source_target_pairs={{2,0},{3,1},{130,128},{131,129},{258,256},{259,257},{386,384},{387... | collective-permute-start | bytes 3145736 | tf_op jit(solution)/shard_map/ppermute | solution.py:46
  74.4 27.3 %collective-permute-start.227 = (bf16[512,1024]{1,0:T(8,128)(2,1)S(1)}, bf16[512,1024]{1,0:T(8,128)(2,1)S(1)}, u32[]{:S(2)}, u32[]{:S(2)}) collective-permute-start(bf16[512,1024]{1,0:T(8,128)(2,1)S(1)} %constant_dynamic-update-slice_fusion.held), channel_id=1, source_target_pairs={{6,0},{7,1},{134,128},{135,129},{262,256},{263,257},{390,384},{391... | collective-permute-start | bytes 3145736 | tf_op jit(solution)/shard_map/ppermute | solution.py:46
  78.7 25.0 %collective-permute-start.223 = (bf16[512,256]{1,0:T(8,128)(2,1)}, bf16[512,256]{1,0:T(8,128)(2,1)}, u32[]{:S(2)}, u32[]{:S(2)}) collective-permute-start(bf16[512,256]{1,0:T(8,128)(2,1)} %pad_maximum_fusion.34), channel_id=1, source_target_pairs={{8,1},{136,129},{264,257},{392,385},{1,8},{129,136},{257,264},{385... | collective-permute-start | bytes 786440 | tf_op jit(solution)/shard_map/ppermute | solution.py:46
  85.3 18.4 %copy-start.10 = (bf16[128,256]{1,0:T(8,128)(2,1)S(1)}, bf16[128,256]{1,0:T(8,128)(2,1)}, u32[]{:S(2)}) copy-start(bf16[128,256]{1,0:T(8,128)(2,1)} %copy-done.9) | copy-start | bytes 196612
  85.3 18.4 %copy-start.12 = (bf16[128,256]{1,0:T(8,128)(2,1)S(1)}, bf16[128,256]{1,0:T(8,128)(2,1)}, u32[]{:S(2)}) copy-start(bf16[128,256]{1,0:T(8,128)(2,1)} %copy-done.11) | copy-start | bytes 196612
  96.4 16.0 %collective-permute-start.230 = (bf16[256,1024]{1,0:T(8,128)(2,1)S(1)}, bf16[256,1024]{1,0:T(8,128)(2,1)S(1)}, u32[]{:S(2)}, u32[]{:S(2)}) collective-permute-start(bf16[256,1024]{1,0:T(8,128)(2,1)S(1)} %slice.285), channel_id=1, source_target_pairs={{2,0},{3,1},{130,128},{131,129},{258,256},{259,257},{386,384},{387... | collective-permute-start | bytes 1572872 | tf_op jit(solution)/shard_map/ppermute | solution.py:46
  101.8 14.9 %collective-permute-start.229 = (bf16[256,1024]{1,0:T(8,128)(2,1)S(1)}, bf16[256,1024]{1,0:T(8,128)(2,1)S(1)}, u32[]{:S(2)}, u32[]{:S(2)}) collective-permute-start(bf16[256,1024]{1,0:T(8,128)(2,1)S(1)} %slice.284), channel_id=1, source_target_pairs={{6,0},{7,1},{134,128},{135,129},{262,256},{263,257},{390,384},{391... | collective-permute-start | bytes 1572872 | tf_op jit(solution)/shard_map/ppermute | solution.py:46
  104.8 4.6 %collective-permute-start.224 = (bf16[512,256]{1,0:T(8,128)(2,1)S(1)}, bf16[512,256]{1,0:T(8,128)(2,1)S(1)}, u32[]{:S(2)}, u32[]{:S(2)}) collective-permute-start(bf16[512,256]{1,0:T(8,128)(2,1)S(1)} %broadcast_select_fusion.2), channel_id=1, source_target_pairs={{1,0},{0,1},{129,128},{128,129},{257,256},{256,257},{385,384},{384... | collective-permute-start | bytes 786440 | tf_op jit(solution)/shard_map/ppermute | solution.py:46
  118.5 6.8 %collective-permute-start.231 = (bf16[2,256,1024]{2,1,0:T(8,128)(2,1)S(1)}, bf16[2,256,1024]{2,1,0:T(8,128)(2,1)S(1)}, u32[]{:S(2)}, u32[]{:S(2)}) collective-permute-start(bf16[2,256,1024]{2,1,0:T(8,128)(2,1)S(1)} %products.3), channel_id=1, source_target_pairs={{1,0},{0,1},{129,128},{128,129},{257,256},{256,257},{385,384},{384... | collective-permute-start | bytes 3145736 | tf_op jit(solution)/shard_map/ppermute | solution.py:46
